TPU v7x, 128 devices: a whole 4x4x4 slice. The times are simulated.
128 devices in a mesh: pipe: 8 (over x, core), ctx: 16 (over y, z).
Axes of the slice: x: 4, y: 4, z: 4, core: 2. Of those that a mesh axis runs over, the one named last changes fastest.
Arguments:
- key_blocks: int32 [1, 16, 3], replicated, may hold values from -1 to 15, as said below
- ranker: int32 [1, 2048], replicated, may hold values from 0 to 1
- section_inputs: bfloat16 [8, 1, 2048, 1024], P('pipe', None, 'ctx'), may hold values from -6 to 6
- output_grad: bfloat16 [1, 2048, 1024], P(None, 'ctx'), may hold values from -6 to 6
- input_proj: bfloat16 [8, 4096, 1024], P('pipe'), may hold values from -0.1875 to 0.1875
- output_proj: bfloat16 [8, 1024, 1024], P('pipe'), may hold values from -0.1875 to 0.1875
- norm_gain: float32 [8, 1024], P('pipe'), may hold values from 0.5 to 1.5
Outputs:
- section_grads: bfloat16 [8, 1, 2048, 1024], P('pipe', None, 'ctx')
- input_proj_grad: float32 [8, 4096, 1024], P('pipe', 'ctx')
Inputs may be any that keep to these rules, and one draw needn't show every extreme that they name: `key_blocks`: row n of history h: slot 0 is n, slot 1 is n - 1, the next slots are distinct earlier blocks; -1 marks unused slots and only follows the used ones. Lists hold 2 to 3 used slots, fewer near the start.
All inputs are finite; a program needn't handle non-finite values.
Results may differ from a plain program's by a relative error of at most 0.034.
Values may be sent and summed in bfloat16 or wider, within the bound.
A program may use at most 128 MiB of HBM per device.

v0:
```python
import jax
import jax.numpy as jnp
from jax import lax
from jax.sharding import PartitionSpec as P

H = 16
BLOCK = 128


def from_behind(x, axis, by):
    peers = lax.axis_size(axis)
    pairs = [(i, i + by) for i in range(peers) if 0 <= i + by < peers]
    return lax.ppermute(x, axis, pairs)


def silu_slope(argument):
    sigma = jax.nn.sigmoid(argument)
    return sigma * (1.0 + argument * (1.0 - sigma))


def build_allowed(blocks, rankers, select_full, block_count):
    length = block_count * BLOCK
    offsets = jnp.arange(BLOCK, dtype=jnp.int32)
    key_pos = blocks[:, :, None] * BLOCK + offsets[None, None, :]
    query_pos = jnp.arange(length, dtype=jnp.int32).reshape(block_count, BLOCK)
    rank_blocks = rankers.reshape(block_count, BLOCK).astype(jnp.float32)
    key_rank = jnp.einsum("nkm,mc->nkc", select_full, rank_blocks)
    live = (blocks >= 0)[:, None, :, None]
    causal = key_pos[:, None, :, :] <= query_pos[:, :, None, None]
    same_rank = key_rank[:, None, :, :] == rank_blocks[:, :, None, None]
    return live & causal & same_rank


def head_backward(projected, cot_gate, gain_heads, blocks, rankers):
    head_count, _, block_count, head_width, block_len = projected.shape
    score_scale = head_width ** (-0.5)
    pre_float = projected.astype(jnp.float32)
    activated = jax.nn.silu(pre_float).astype(jnp.bfloat16)
    gate_act = activated[:, 0]
    value_act = activated[:, 1]
    query_act = activated[:, 2]
    key_act = activated[:, 3]
    select = blocks[:, :, None] == jnp.arange(block_count, dtype=jnp.int32)[None, None, :]
    select_half = select.astype(jnp.bfloat16)
    select_full = select.astype(jnp.float32)
    key_tiles = jnp.einsum(
        "nkm,hmjc->hnkjc", select_half, key_act, preferred_element_type=jnp.float32
    ).astype(jnp.bfloat16)
    value_tiles = jnp.einsum(
        "nkm,hmjc->hnkjc", select_half, value_act, preferred_element_type=jnp.float32
    ).astype(jnp.bfloat16)
    allowed = build_allowed(blocks, rankers, select_full, block_count)[None]
    scores = (
        jnp.einsum("hnjq,hnkjc->hnqkc", query_act, key_tiles, preferred_element_type=jnp.float32)
        * score_scale
    )
    weights = jnp.where(allowed, jax.nn.silu(scores), 0.0).astype(jnp.bfloat16)
    attended = jnp.einsum(
        "hnqkc,hnkjc->hnjq", weights, value_tiles, preferred_element_type=jnp.float32
    )
    inv_rms = lax.rsqrt(jnp.mean(attended * attended, axis=2, keepdims=True) + 1.0)
    normed = attended * inv_rms
    scaled = cot_gate.astype(jnp.float32) * gain_heads[:, None, :, None]
    grad_gate = scaled * normed
    grad_normed = scaled * gate_act.astype(jnp.float32)
    grad_attended = (
        inv_rms * (grad_normed - normed * jnp.mean(grad_normed * normed, axis=2, keepdims=True))
    ).astype(jnp.bfloat16)
    grad_weights = jnp.einsum(
        "hnjq,hnkjc->hnqkc", grad_attended, value_tiles, preferred_element_type=jnp.float32
    )
    value_tile_grads = jnp.einsum(
        "hnqkc,hnjq->hnkjc", weights, grad_attended, preferred_element_type=jnp.float32
    )
    grad_value = jnp.einsum(
        "nkm,hnkjc->hmjc", select_full, value_tile_grads, precision=lax.Precision.HIGHEST
    )
    grad_scores = (grad_weights * jnp.where(allowed, silu_slope(scores), 0.0) * score_scale).astype(
        jnp.bfloat16
    )
    grad_query = jnp.einsum(
        "hnqkc,hnkjc->hnjq", grad_scores, key_tiles, preferred_element_type=jnp.float32
    )
    key_tile_grads = jnp.einsum(
        "hnqkc,hnjq->hnkjc", grad_scores, query_act, preferred_element_type=jnp.float32
    )
    grad_key = jnp.einsum(
        "nkm,hnkjc->hmjc", select_full, key_tile_grads, precision=lax.Precision.HIGHEST
    )
    grad_parts = jnp.stack([grad_gate, grad_value, grad_query, grad_key], axis=1)
    return (grad_parts * silu_slope(pre_float)).astype(jnp.bfloat16)


def place_entry(buffer, hist_slot, updated, active):
    previous = lax.dynamic_index_in_dim(buffer, hist_slot, 0, keepdims=False)
    chosen = jnp.where(active, updated, previous)
    return lax.dynamic_update_index_in_dim(buffer, chosen, hist_slot, 0)


def per_device(key_blocks, ranker, section_inputs, output_grad, input_proj, output_proj, norm_gain):
    local_inputs = section_inputs[0]
    ctx_count = lax.axis_size("ctx")
    pipe_count = lax.axis_size("pipe")
    section_pos = lax.axis_index("pipe")
    ctx_pos = lax.axis_index("ctx")
    seq_count, events, width_all = local_inputs.shape
    head_width = width_all // H
    local_heads = H // ctx_count
    length = events * ctx_count
    row_count = 4 * width_all // ctx_count
    local_blocks = events // BLOCK
    weight_four = input_proj[0].reshape(H, 4, head_width, width_all)
    weight_out = output_proj[0].reshape(width_all, H, head_width)
    inputs_blocks = local_inputs.reshape(seq_count, local_blocks, BLOCK, width_all)
    grads_blocks = output_grad.reshape(seq_count, local_blocks, BLOCK, width_all)
    gain_here = lax.dynamic_slice_in_dim(
        norm_gain[0], ctx_pos * local_heads * head_width, local_heads * head_width
    )
    gain_here = gain_here.reshape(local_heads, head_width)
    saved_init = jnp.zeros((seq_count, H, 4, local_blocks, head_width, BLOCK), jnp.bfloat16)

    def tick_step(tick_index, state_carry):
        incoming, grads_buffer, saved = state_carry
        history = tick_index - (pipe_count - 1 - section_pos)
        active = (history >= 0) & (history < seq_count)
        hist_slot = jnp.clip(history, 0, seq_count - 1)
        inputs_now = lax.dynamic_index_in_dim(inputs_blocks, hist_slot, 0, keepdims=False)
        top_grad = lax.dynamic_index_in_dim(grads_blocks, hist_slot, 0, keepdims=False)
        upstream = jnp.where(section_pos == pipe_count - 1, top_grad, incoming)
        projected = jnp.einsum(
            "hpjd,ncd->hpnjc", weight_four, inputs_now, preferred_element_type=jnp.float32
        ).astype(jnp.bfloat16)
        proj_heads = lax.all_to_all(projected, "ctx", split_axis=0, concat_axis=2, tiled=True)
        cot_gate = jnp.einsum(
            "ncd,dhj->hnjc", upstream, weight_out, preferred_element_type=jnp.float32
        ).astype(jnp.bfloat16)
        cot_heads = lax.all_to_all(cot_gate, "ctx", split_axis=0, concat_axis=1, tiled=True)
        blocks_now = lax.dynamic_index_in_dim(key_blocks, hist_slot, 0, keepdims=False)
        ranks_now = lax.dynamic_index_in_dim(ranker, hist_slot, 0, keepdims=False)
        grad_heads = head_backward(proj_heads, cot_heads, gain_here, blocks_now, ranks_now)
        grad_events = lax.all_to_all(grad_heads, "ctx", split_axis=2, concat_axis=0, tiled=True)
        section_grad = upstream.astype(jnp.float32) + jnp.einsum(
            "hpnjc,hpjd->ncd", grad_events, weight_four, preferred_element_type=jnp.float32
        )
        section_grad = section_grad.astype(jnp.bfloat16)
        grads_buffer = place_entry(grads_buffer, hist_slot, section_grad, active)
        saved = place_entry(saved, hist_slot, grad_events, active)
        incoming = from_behind(section_grad, "pipe", -1)
        return (incoming, grads_buffer, saved)

    start_state = (
        jnp.zeros((local_blocks, BLOCK, width_all), jnp.bfloat16),
        jnp.zeros((seq_count, local_blocks, BLOCK, width_all), jnp.bfloat16),
        saved_init,
    )
    _, grads_buffer, saved = lax.fori_loop(0, seq_count + pipe_count - 1, tick_step, start_state)
    norm_factor = float(seq_count * length) ** (-0.5)
    term = jnp.einsum("shpnjc,sncd->hpjd", saved, inputs_blocks, preferred_element_type=jnp.float32)
    summed = lax.psum_scatter(
        term.reshape(lax.axis_size("ctx") * row_count, width_all).astype(jnp.bfloat16),
        "ctx",
        scatter_dimension=0,
        tiled=True,
    ).astype(jnp.float32)
    return (grads_buffer.reshape(seq_count, events, width_all)[None], (summed * norm_factor)[None])


def solution(mesh):
    placed = (
        P(),
        P(),
        P("pipe", None, "ctx", None),
        P(None, "ctx", None),
        P("pipe", None, None),
        P("pipe", None, None),
        P("pipe", None),
    )
    return jax.shard_map(
        per_device,
        mesh=mesh,
        in_specs=placed,
        out_specs=(P("pipe", None, "ctx", None), P("pipe", "ctx", None)),
        check_vma=False,
    )
```

profile of v0, /device:TPU:0, one launch (start us, length us, event | category | flops | bytes accessed | tf_op | source)
XLA Modules:
  0.0 686.9 jit_solution(7259673593508570541)
XLA Ops:
  8.1 6.7 fusion.49
  14.8 8.3 %all-to-all-start.2 = ((bf16[16,4,1,64,128]{4,3,1,2,0:T(8,128)(2,1)}), bf16[16,4,1,64,128]{4,3,1,2,0:T(8,128)(2,1)S(1)}, u32[]{:S(2)}, u32[]{:S(2)}) async-start(bf16[16,4,1,64,128]{4,3,1,2,0:T(8,128)(2,1)} %fusion.49), calls=%async_computation.2 | async-start | bytes 2097152 | tf_op jit(solution)/shard_map/while/body/eval_jaxpr/all_to_all | solution.py:133
  26.6 14.2 %all-to-all-done.2 = bf16[16,4,1,64,128]{4,3,1,2,0:T(8,128)(2,1)S(1)} async-done(((bf16[16,4,1,64,128]{4,3,1,2,0:T(8,128)(2,1)}), bf16[16,4,1,64,128]{4,3,1,2,0:T(8,128)(2,1)S(1)}, u32[]{:S(2)}, u32[]{:S(2)}) %all-to-all-start.2) | async-done | bytes 1048608 | tf_op jit(solution)/shard_map/while/body/eval_jaxpr/all_to_all | solution.py:133
  44.0 527.1 %while.20 = (s32[]{:T(128)}, bf16[1,128,1024]{2,1,0:T(8,128)(2,1)}, bf16[1,1,128,1024]{3,2,1,0:T(8,128)(2,1)}, bf16[1,16,4,1,64,128]{5,4,2,1,3,0:T(8,128)(2,1)},...) while((s32[]{:T(128)}, bf16[1,128,1024]{2,1,0:T(8,128)(2,1)}, ...), condition=%wide.region_3.4_spmd.clone, body=%wide.region_0.3_spmd.clone.sunk | while | flops 2158968832 | bytes 99150752 | solution.py:156
  76.1 7.1 %all-to-all-start.1 = ((bf16[1,4,16,64,128]{4,3,1,0,2:T(8,128)(2,1)}), bf16[1,4,16,64,128]{4,3,1,0,2:T(8,128)(2,1)S(1)}, u32[]{:S(2)}, u32[]{:S(2)}) async-start(bf16[1,4,16,64,128]{4,3,1,0,2:T(8,128)(2,1)} %copy.181), calls=%async_computation.1 | async-start | bytes 2097152 | tf_op jit(solution)/shard_map/while/body/eval_jaxpr/all_to_all | solution.py:141
  83.2 14.3 %all-to-all-done.1 = bf16[1,4,16,64,128]{4,3,1,0,2:T(8,128)(2,1)S(1)} async-done(((bf16[1,4,16,64,128]{4,3,1,0,2:T(8,128)(2,1)}), bf16[1,4,16,64,128]{4,3,1,0,2:T(8,128)(2,1)S(1)}, u32[]{:S(2)}, u32[]{:S(2)}) %all-to-all-start.1) | async-done | bytes 1048608 | tf_op jit(solution)/shard_map/while/body/eval_jaxpr/all_to_all | solution.py:141
  97.5 4.8 fusion.122
  138.0 7.1 %all-to-all-start.1 = ((bf16[1,4,16,64,128]{4,3,1,0,2:T(8,128)(2,1)}), bf16[1,4,16,64,128]{4,3,1,0,2:T(8,128)(2,1)S(1)}, u32[]{:S(2)}, u32[]{:S(2)}) async-start(bf16[1,4,16,64,128]{4,3,1,0,2:T(8,128)(2,1)} %copy.181), calls=%async_computation.1 | async-start | bytes 2097152 | tf_op jit(solution)/shard_map/while/body/eval_jaxpr/all_to_all | solution.py:141
  145.1 15.9 %all-to-all-done.1 = bf16[1,4,16,64,128]{4,3,1,0,2:T(8,128)(2,1)S(1)} async-done(((bf16[1,4,16,64,128]{4,3,1,0,2:T(8,128)(2,1)}), bf16[1,4,16,64,128]{4,3,1,0,2:T(8,128)(2,1)S(1)}, u32[]{:S(2)}, u32[]{:S(2)}) %all-to-all-start.1) | async-done | bytes 1048608 | tf_op jit(solution)/shard_map/while/body/eval_jaxpr/all_to_all | solution.py:141
  161.0 4.8 fusion.122
  203.4 7.1 %all-to-all-start.1 = ((bf16[1,4,16,64,128]{4,3,1,0,2:T(8,128)(2,1)}), bf16[1,4,16,64,128]{4,3,1,0,2:T(8,128)(2,1)S(1)}, u32[]{:S(2)}, u32[]{:S(2)}) async-start(bf16[1,4,16,64,128]{4,3,1,0,2:T(8,128)(2,1)} %copy.181), calls=%async_computation.1 | async-start | bytes 2097152 | tf_op jit(solution)/shard_map/while/body/eval_jaxpr/all_to_all | solution.py:141
  210.5 13.0 %all-to-all-done.1 = bf16[1,4,16,64,128]{4,3,1,0,2:T(8,128)(2,1)S(1)} async-done(((bf16[1,4,16,64,128]{4,3,1,0,2:T(8,128)(2,1)}), bf16[1,4,16,64,128]{4,3,1,0,2:T(8,128)(2,1)S(1)}, u32[]{:S(2)}, u32[]{:S(2)}) %all-to-all-start.1) | async-done | bytes 1048608 | tf_op jit(solution)/shard_map/while/body/eval_jaxpr/all_to_all | solution.py:141
  231.7 5.6 collective-permute-done
  269.4 7.1 %all-to-all-start.1 = ((bf16[1,4,16,64,128]{4,3,1,0,2:T(8,128)(2,1)}), bf16[1,4,16,64,128]{4,3,1,0,2:T(8,128)(2,1)S(1)}, u32[]{:S(2)}, u32[]{:S(2)}) async-start(bf16[1,4,16,64,128]{4,3,1,0,2:T(8,128)(2,1)} %copy.181), calls=%async_computation.1 | async-start | bytes 2097152 | tf_op jit(solution)/shard_map/while/body/eval_jaxpr/all_to_all | solution.py:141
  276.5 12.9 %all-to-all-done.1 = bf16[1,4,16,64,128]{4,3,1,0,2:T(8,128)(2,1)S(1)} async-done(((bf16[1,4,16,64,128]{4,3,1,0,2:T(8,128)(2,1)}), bf16[1,4,16,64,128]{4,3,1,0,2:T(8,128)(2,1)S(1)}, u32[]{:S(2)}, u32[]{:S(2)}) %all-to-all-start.1) | async-done | bytes 1048608 | tf_op jit(solution)/shard_map/while/body/eval_jaxpr/all_to_all | solution.py:141
  297.6 8.0 %collective-permute-done = bf16[1,128,1024]{2,1,0:T(8,128)(2,1)} collective-permute-done((bf16[1,128,1024]{2,1,0:T(8,128)(2,1)S(1)}, bf16[1,128,1024]{2,1,0:T(8,128)(2,1)}, u32[]{:S(2)}, u32[]{:S(2)}) %collective-permute-start) | collective-permute-done | bytes 262176 | tf_op jit(solution)/shard_map/while/body/eval_jaxpr/ppermute | solution.py:13
  337.7 7.1 %all-to-all-start.1 = ((bf16[1,4,16,64,128]{4,3,1,0,2:T(8,128)(2,1)}), bf16[1,4,16,64,128]{4,3,1,0,2:T(8,128)(2,1)S(1)}, u32[]{:S(2)}, u32[]{:S(2)}) async-start(bf16[1,4,16,64,128]{4,3,1,0,2:T(8,128)(2,1)} %copy.181), calls=%async_computation.1 | async-start | bytes 2097152 | tf_op jit(solution)/shard_map/while/body/eval_jaxpr/all_to_all | solution.py:141
  344.9 13.0 %all-to-all-done.1 = bf16[1,4,16,64,128]{4,3,1,0,2:T(8,128)(2,1)S(1)} async-done(((bf16[1,4,16,64,128]{4,3,1,0,2:T(8,128)(2,1)}), bf16[1,4,16,64,128]{4,3,1,0,2:T(8,128)(2,1)S(1)}, u32[]{:S(2)}, u32[]{:S(2)}) %all-to-all-start.1) | async-done | bytes 1048608 | tf_op jit(solution)/shard_map/while/body/eval_jaxpr/all_to_all | solution.py:141
  366.0 6.4 collective-permute-done
  404.6 7.1 %all-to-all-start.1 = ((bf16[1,4,16,64,128]{4,3,1,0,2:T(8,128)(2,1)}), bf16[1,4,16,64,128]{4,3,1,0,2:T(8,128)(2,1)S(1)}, u32[]{:S(2)}, u32[]{:S(2)}) async-start(bf16[1,4,16,64,128]{4,3,1,0,2:T(8,128)(2,1)} %copy.181), calls=%async_computation.1 | async-start | bytes 2097152 | tf_op jit(solution)/shard_map/while/body/eval_jaxpr/all_to_all | solution.py:141
  411.7 13.0 %all-to-all-done.1 = bf16[1,4,16,64,128]{4,3,1,0,2:T(8,128)(2,1)S(1)} async-done(((bf16[1,4,16,64,128]{4,3,1,0,2:T(8,128)(2,1)}), bf16[1,4,16,64,128]{4,3,1,0,2:T(8,128)(2,1)S(1)}, u32[]{:S(2)}, u32[]{:S(2)}) %all-to-all-start.1) | async-done | bytes 1048608 | tf_op jit(solution)/shard_map/while/body/eval_jaxpr/all_to_all | solution.py:141
  424.7 4.8 fusion.122
  433.0 6.6 collective-permute-done
  471.6 7.1 %all-to-all-start.1 = ((bf16[1,4,16,64,128]{4,3,1,0,2:T(8,128)(2,1)}), bf16[1,4,16,64,128]{4,3,1,0,2:T(8,128)(2,1)S(1)}, u32[]{:S(2)}, u32[]{:S(2)}) async-start(bf16[1,4,16,64,128]{4,3,1,0,2:T(8,128)(2,1)} %copy.181), calls=%async_computation.1 | async-start | bytes 2097152 | tf_op jit(solution)/shard_map/while/body/eval_jaxpr/all_to_all | solution.py:141
  478.7 13.0 %all-to-all-done.1 = bf16[1,4,16,64,128]{4,3,1,0,2:T(8,128)(2,1)S(1)} async-done(((bf16[1,4,16,64,128]{4,3,1,0,2:T(8,128)(2,1)}), bf16[1,4,16,64,128]{4,3,1,0,2:T(8,128)(2,1)S(1)}, u32[]{:S(2)}, u32[]{:S(2)}) %all-to-all-start.1) | async-done | bytes 1048608 | tf_op jit(solution)/shard_map/while/body/eval_jaxpr/all_to_all | solution.py:141
  491.7 4.8 fusion.122
  500.0 5.7 collective-permute-done
  537.8 7.1 %all-to-all-start.1 = ((bf16[1,4,16,64,128]{4,3,1,0,2:T(8,128)(2,1)}), bf16[1,4,16,64,128]{4,3,1,0,2:T(8,128)(2,1)S(1)}, u32[]{:S(2)}, u32[]{:S(2)}) async-start(bf16[1,4,16,64,128]{4,3,1,0,2:T(8,128)(2,1)} %copy.181), calls=%async_computation.1 | async-start | bytes 2097152 | tf_op jit(solution)/shard_map/while/body/eval_jaxpr/all_to_all | solution.py:141
  544.9 13.0 %all-to-all-done.1 = bf16[1,4,16,64,128]{4,3,1,0,2:T(8,128)(2,1)S(1)} async-done(((bf16[1,4,16,64,128]{4,3,1,0,2:T(8,128)(2,1)}), bf16[1,4,16,64,128]{4,3,1,0,2:T(8,128)(2,1)S(1)}, u32[]{:S(2)}, u32[]{:S(2)}) %all-to-all-start.1) | async-done | bytes 1048608 | tf_op jit(solution)/shard_map/while/body/eval_jaxpr/all_to_all | solution.py:141
  566.0 5.1 collective-permute-done
  571.1 6.8 convolution_convert_fusion.2
  577.9 100.0 %reduce-scatter.2.cloned.1.call-done = bf16[256,1024]{1,0:T(8,128)(2,1)} async-done(((bf16[4096,1024]{1,0:T(8,128)(2,1)}), bf16[256,1024]{1,0:T(8,128)(2,1)}) %reduce-scatter.2.cloned.1.call-update) | async-done | bytes 524304 | tf_op jit(solution)/shard_map/reduce_scatter | solution.py:159
  (426 shorter events, 313.6 us)
Async XLA Ops:
  14.8 8.4 %copy-start.9 = (s32[1,2048]{1,0:T(1,128)S(1)}, s32[1,2048]{1,0:T(1,128)}, u32[]{:S(2)}) copy-start(s32[1,2048]{1,0:T(1,128)} %param.10) | copy-start | bytes 24580
  14.8 8.4 %copy-start.8 = (bf16[1,1024,1024]{2,1,0:T(8,128)(2,1)S(1)}, bf16[1,1024,1024]{2,1,0:T(8,128)(2,1)}, u32[]{:S(2)}) copy-start(bf16[1,1024,1024]{2,1,0:T(8,128)(2,1)} %param.14) | copy-start | bytes 6291460
  14.8 26.0 %all-to-all-start.2 = ((bf16[16,4,1,64,128]{4,3,1,2,0:T(8,128)(2,1)}), bf16[16,4,1,64,128]{4,3,1,2,0:T(8,128)(2,1)S(1)}, u32[]{:S(2)}, u32[]{:S(2)}) async-start(bf16[16,4,1,64,128]{4,3,1,2,0:T(8,128)(2,1)} %fusion.49), calls=%async_computation.2 | async-start | bytes 2097152 | tf_op jit(solution)/shard_map/while/body/eval_jaxpr/all_to_all | solution.py:133
  23.1 654.8 %reduce-scatter.2.cloned.1.call-start = ((), (), s32[]{:S(2)}) async-start(), calls=%async_computation.4 | async-start | bytes 8912896 | tf_op jit(solution)/shard_map/reduce_scatter | solution.py:159
  47.2 14.3 %all-to-all-start = ((bf16[16,1,64,128]{3,2,1,0:T(8,128)(2,1)}), bf16[16,1,64,128]{3,2,1,0:T(8,128)(2,1)}, u32[]{:S(2)}, u32[]{:S(2)}) async-start(bf16[16,1,64,128]{3,2,1,0:T(8,128)(2,1)} %convert_bitcast_fusion.2), calls=%async_computation | async-start | bytes 524288 | tf_op jit(solution)/shard_map/while/body/eval_jaxpr/all_to_all | solution.py:137
  76.1 21.5 %all-to-all-start.1 = ((bf16[1,4,16,64,128]{4,3,1,0,2:T(8,128)(2,1)}), bf16[1,4,16,64,128]{4,3,1,0,2:T(8,128)(2,1)S(1)}, u32[]{:S(2)}, u32[]{:S(2)}) async-start(bf16[1,4,16,64,128]{4,3,1,0,2:T(8,128)(2,1)} %copy.181), calls=%async_computation.1 | async-start | bytes 2097152 | tf_op jit(solution)/shard_map/while/body/eval_jaxpr/all_to_all | solution.py:141
  102.3 3.6 collective-permute-start
  109.1 14.3 %all-to-all-start = ((bf16[16,1,64,128]{3,2,1,0:T(8,128)(2,1)}), bf16[16,1,64,128]{3,2,1,0:T(8,128)(2,1)}, u32[]{:S(2)}, u32[]{:S(2)}) async-start(bf16[16,1,64,128]{3,2,1,0:T(8,128)(2,1)} %convert_bitcast_fusion.2), calls=%async_computation | async-start | bytes 524288 | tf_op jit(solution)/shard_map/while/body/eval_jaxpr/all_to_all | solution.py:137
  138.0 23.0 %all-to-all-start.1 = ((bf16[1,4,16,64,128]{4,3,1,0,2:T(8,128)(2,1)}), bf16[1,4,16,64,128]{4,3,1,0,2:T(8,128)(2,1)S(1)}, u32[]{:S(2)}, u32[]{:S(2)}) async-start(bf16[1,4,16,64,128]{4,3,1,0,2:T(8,128)(2,1)} %copy.181), calls=%async_computation.1 | async-start | bytes 2097152 | tf_op jit(solution)/shard_map/while/body/eval_jaxpr/all_to_all | solution.py:141
  165.8 5.5 collective-permute-start
  174.5 14.3 %all-to-all-start = ((bf16[16,1,64,128]{3,2,1,0:T(8,128)(2,1)}), bf16[16,1,64,128]{3,2,1,0:T(8,128)(2,1)}, u32[]{:S(2)}, u32[]{:S(2)}) async-start(bf16[16,1,64,128]{3,2,1,0:T(8,128)(2,1)} %convert_bitcast_fusion.2), calls=%async_computation | async-start | bytes 524288 | tf_op jit(solution)/shard_map/while/body/eval_jaxpr/all_to_all | solution.py:137
  203.4 20.1 %all-to-all-start.1 = ((bf16[1,4,16,64,128]{4,3,1,0,2:T(8,128)(2,1)}), bf16[1,4,16,64,128]{4,3,1,0,2:T(8,128)(2,1)S(1)}, u32[]{:S(2)}, u32[]{:S(2)}) async-start(bf16[1,4,16,64,128]{4,3,1,0,2:T(8,128)(2,1)} %copy.181), calls=%async_computation.1 | async-start | bytes 2097152 | tf_op jit(solution)/shard_map/while/body/eval_jaxpr/all_to_all | solution.py:141
  228.3 9.0 %collective-permute-start = (bf16[1,128,1024]{2,1,0:T(8,128)(2,1)S(1)}, bf16[1,128,1024]{2,1,0:T(8,128)(2,1)}, u32[]{:S(2)}, u32[]{:S(2)}) collective-permute-start(bf16[1,128,1024]{2,1,0:T(8,128)(2,1)S(1)} %fusion.122), channel_id=1, source_target_pairs={{16,0},{32,16},{48,32},{64,48},{80,64},{96,80},{112,96},{17,1},{33... | collective-permute-start | bytes 786440 | tf_op jit(solution)/shard_map/while/body/eval_jaxpr/ppermute | solution.py:13
  240.5 14.3 %all-to-all-start = ((bf16[16,1,64,128]{3,2,1,0:T(8,128)(2,1)}), bf16[16,1,64,128]{3,2,1,0:T(8,128)(2,1)}, u32[]{:S(2)}, u32[]{:S(2)}) async-start(bf16[16,1,64,128]{3,2,1,0:T(8,128)(2,1)} %convert_bitcast_fusion.2), calls=%async_computation | async-start | bytes 524288 | tf_op jit(solution)/shard_map/while/body/eval_jaxpr/all_to_all | solution.py:137
  269.4 20.0 %all-to-all-start.1 = ((bf16[1,4,16,64,128]{4,3,1,0,2:T(8,128)(2,1)}), bf16[1,4,16,64,128]{4,3,1,0,2:T(8,128)(2,1)S(1)}, u32[]{:S(2)}, u32[]{:S(2)}) async-start(bf16[1,4,16,64,128]{4,3,1,0,2:T(8,128)(2,1)} %copy.181), calls=%async_computation.1 | async-start | bytes 2097152 | tf_op jit(solution)/shard_map/while/body/eval_jaxpr/all_to_all | solution.py:141
  294.2 11.4 %collective-permute-start = (bf16[1,128,1024]{2,1,0:T(8,128)(2,1)S(1)}, bf16[1,128,1024]{2,1,0:T(8,128)(2,1)}, u32[]{:S(2)}, u32[]{:S(2)}) collective-permute-start(bf16[1,128,1024]{2,1,0:T(8,128)(2,1)S(1)} %fusion.122), channel_id=1, source_target_pairs={{16,0},{32,16},{48,32},{64,48},{80,64},{96,80},{112,96},{17,1},{33... | collective-permute-start | bytes 786440 | tf_op jit(solution)/shard_map/while/body/eval_jaxpr/ppermute | solution.py:13
  295.7 9.9 %copy-start.5 = (bf16[1,16,4,1,64,128]{5,4,2,1,3,0:T(8,128)(2,1)}, bf16[1,16,4,1,64,128]{5,4,2,1,3,0:T(8,128)(2,1)S(1)}, u32[]{:S(2)}) copy-start(bf16[1,16,4,1,64,128]{5,4,2,1,3,0:T(8,128)(2,1)S(1)} %bitcast_select_fusion.5) | copy-start | bytes 3145732 | tf_op jit(solution)/shard_map/while
  308.9 14.3 %all-to-all-start = ((bf16[16,1,64,128]{3,2,1,0:T(8,128)(2,1)}), bf16[16,1,64,128]{3,2,1,0:T(8,128)(2,1)}, u32[]{:S(2)}, u32[]{:S(2)}) async-start(bf16[16,1,64,128]{3,2,1,0:T(8,128)(2,1)} %convert_bitcast_fusion.2), calls=%async_computation | async-start | bytes 524288 | tf_op jit(solution)/shard_map/while/body/eval_jaxpr/all_to_all | solution.py:137
  337.7 20.1 %all-to-all-start.1 = ((bf16[1,4,16,64,128]{4,3,1,0,2:T(8,128)(2,1)}), bf16[1,4,16,64,128]{4,3,1,0,2:T(8,128)(2,1)S(1)}, u32[]{:S(2)}, u32[]{:S(2)}) async-start(bf16[1,4,16,64,128]{4,3,1,0,2:T(8,128)(2,1)} %copy.181), calls=%async_computation.1 | async-start | bytes 2097152 | tf_op jit(solution)/shard_map/while/body/eval_jaxpr/all_to_all | solution.py:141
  362.6 9.9 %collective-permute-start = (bf16[1,128,1024]{2,1,0:T(8,128)(2,1)S(1)}, bf16[1,128,1024]{2,1,0:T(8,128)(2,1)}, u32[]{:S(2)}, u32[]{:S(2)}) collective-permute-start(bf16[1,128,1024]{2,1,0:T(8,128)(2,1)S(1)} %fusion.122), channel_id=1, source_target_pairs={{16,0},{32,16},{48,32},{64,48},{80,64},{96,80},{112,96},{17,1},{33... | collective-permute-start | bytes 786440 | tf_op jit(solution)/shard_map/while/body/eval_jaxpr/ppermute | solution.py:13
  364.1 8.3 %copy-start.5 = (bf16[1,16,4,1,64,128]{5,4,2,1,3,0:T(8,128)(2,1)}, bf16[1,16,4,1,64,128]{5,4,2,1,3,0:T(8,128)(2,1)S(1)}, u32[]{:S(2)}) copy-start(bf16[1,16,4,1,64,128]{5,4,2,1,3,0:T(8,128)(2,1)S(1)} %bitcast_select_fusion.5) | copy-start | bytes 3145732 | tf_op jit(solution)/shard_map/while
  375.7 14.3 %all-to-all-start = ((bf16[16,1,64,128]{3,2,1,0:T(8,128)(2,1)}), bf16[16,1,64,128]{3,2,1,0:T(8,128)(2,1)}, u32[]{:S(2)}, u32[]{:S(2)}) async-start(bf16[16,1,64,128]{3,2,1,0:T(8,128)(2,1)} %convert_bitcast_fusion.2), calls=%async_computation | async-start | bytes 524288 | tf_op jit(solution)/shard_map/while/body/eval_jaxpr/all_to_all | solution.py:137
  404.6 20.2 %all-to-all-start.1 = ((bf16[1,4,16,64,128]{4,3,1,0,2:T(8,128)(2,1)}), bf16[1,4,16,64,128]{4,3,1,0,2:T(8,128)(2,1)S(1)}, u32[]{:S(2)}, u32[]{:S(2)}) async-start(bf16[1,4,16,64,128]{4,3,1,0,2:T(8,128)(2,1)} %copy.181), calls=%async_computation.1 | async-start | bytes 2097152 | tf_op jit(solution)/shard_map/while/body/eval_jaxpr/all_to_all | solution.py:141
  429.5 10.0 %collective-permute-start = (bf16[1,128,1024]{2,1,0:T(8,128)(2,1)S(1)}, bf16[1,128,1024]{2,1,0:T(8,128)(2,1)}, u32[]{:S(2)}, u32[]{:S(2)}) collective-permute-start(bf16[1,128,1024]{2,1,0:T(8,128)(2,1)S(1)} %fusion.122), channel_id=1, source_target_pairs={{16,0},{32,16},{48,32},{64,48},{80,64},{96,80},{112,96},{17,1},{33... | collective-permute-start | bytes 786440 | tf_op jit(solution)/shard_map/while/body/eval_jaxpr/ppermute | solution.py:13
  431.1 8.5 %copy-start.5 = (bf16[1,16,4,1,64,128]{5,4,2,1,3,0:T(8,128)(2,1)}, bf16[1,16,4,1,64,128]{5,4,2,1,3,0:T(8,128)(2,1)S(1)}, u32[]{:S(2)}) copy-start(bf16[1,16,4,1,64,128]{5,4,2,1,3,0:T(8,128)(2,1)S(1)} %bitcast_select_fusion.5) | copy-start | bytes 3145732 | tf_op jit(solution)/shard_map/while
  442.8 14.3 %all-to-all-start = ((bf16[16,1,64,128]{3,2,1,0:T(8,128)(2,1)}), bf16[16,1,64,128]{3,2,1,0:T(8,128)(2,1)}, u32[]{:S(2)}, u32[]{:S(2)}) async-start(bf16[16,1,64,128]{3,2,1,0:T(8,128)(2,1)} %convert_bitcast_fusion.2), calls=%async_computation | async-start | bytes 524288 | tf_op jit(solution)/shard_map/while/body/eval_jaxpr/all_to_all | solution.py:137
  471.6 20.1 %all-to-all-start.1 = ((bf16[1,4,16,64,128]{4,3,1,0,2:T(8,128)(2,1)}), bf16[1,4,16,64,128]{4,3,1,0,2:T(8,128)(2,1)S(1)}, u32[]{:S(2)}, u32[]{:S(2)}) async-start(bf16[1,4,16,64,128]{4,3,1,0,2:T(8,128)(2,1)} %copy.181), calls=%async_computation.1 | async-start | bytes 2097152 | tf_op jit(solution)/shard_map/while/body/eval_jaxpr/all_to_all | solution.py:141
  496.5 9.1 %collective-permute-start = (bf16[1,128,1024]{2,1,0:T(8,128)(2,1)S(1)}, bf16[1,128,1024]{2,1,0:T(8,128)(2,1)}, u32[]{:S(2)}, u32[]{:S(2)}) collective-permute-start(bf16[1,128,1024]{2,1,0:T(8,128)(2,1)S(1)} %fusion.122), channel_id=1, source_target_pairs={{16,0},{32,16},{48,32},{64,48},{80,64},{96,80},{112,96},{17,1},{33... | collective-permute-start | bytes 786440 | tf_op jit(solution)/shard_map/while/body/eval_jaxpr/ppermute | solution.py:13
  498.1 7.6 %copy-start.5 = (bf16[1,16,4,1,64,128]{5,4,2,1,3,0:T(8,128)(2,1)}, bf16[1,16,4,1,64,128]{5,4,2,1,3,0:T(8,128)(2,1)S(1)}, u32[]{:S(2)}) copy-start(bf16[1,16,4,1,64,128]{5,4,2,1,3,0:T(8,128)(2,1)S(1)} %bitcast_select_fusion.5) | copy-start | bytes 3145732 | tf_op jit(solution)/shard_map/while
  508.9 14.3 %all-to-all-start = ((bf16[16,1,64,128]{3,2,1,0:T(8,128)(2,1)}), bf16[16,1,64,128]{3,2,1,0:T(8,128)(2,1)}, u32[]{:S(2)}, u32[]{:S(2)}) async-start(bf16[16,1,64,128]{3,2,1,0:T(8,128)(2,1)} %convert_bitcast_fusion.2), calls=%async_computation | async-start | bytes 524288 | tf_op jit(solution)/shard_map/while/body/eval_jaxpr/all_to_all | solution.py:137
  537.8 20.1 %all-to-all-start.1 = ((bf16[1,4,16,64,128]{4,3,1,0,2:T(8,128)(2,1)}), bf16[1,4,16,64,128]{4,3,1,0,2:T(8,128)(2,1)S(1)}, u32[]{:S(2)}, u32[]{:S(2)}) async-start(bf16[1,4,16,64,128]{4,3,1,0,2:T(8,128)(2,1)} %copy.181), calls=%async_computation.1 | async-start | bytes 2097152 | tf_op jit(solution)/shard_map/while/body/eval_jaxpr/all_to_all | solution.py:141
  562.6 8.5 %collective-permute-start = (bf16[1,128,1024]{2,1,0:T(8,128)(2,1)S(1)}, bf16[1,128,1024]{2,1,0:T(8,128)(2,1)}, u32[]{:S(2)}, u32[]{:S(2)}) collective-permute-start(bf16[1,128,1024]{2,1,0:T(8,128)(2,1)S(1)} %fusion.122), channel_id=1, source_target_pairs={{16,0},{32,16},{48,32},{64,48},{80,64},{96,80},{112,96},{17,1},{33... | collective-permute-start | bytes 786440 | tf_op jit(solution)/shard_map/while/body/eval_jaxpr/ppermute | solution.py:13
  (62 other events, 230.9 us)
Sparse Core Ops, SparseCore 0:
  578.0 99.7 reduce-scatter.1
where the time goes:
time: 691 us; the launch traced here: 687 us
  waiting for transfers between devices  262 us (38%)
  matrix products  195 us (28%)
  starting transfers between devices  109 us (16%)
  other arithmetic  80.2 us (12%)
  local copies, waits for them, and re-layouts  24.5 us (4%)
  between operations  14.1 us (2%)
    all_to_all x8, waiting for transfers between devices, tick_step(): lax.all_to_all(grad_heads, 'ctx', split_axis=2, concat_axis=0, tiled=True)  108 us
    reduce_scatter x1, waiting for transfers between devices, per_device(): lax.psum_scatter(term.reshape(lax.axis_size('ctx') * row_count, width_all...  100 us
    all_to_all x8, starting transfers between devices, tick_step(): lax.all_to_all(grad_heads, 'ctx', split_axis=2, concat_axis=0, tiled=True)  56.7 us
    ppermute x8, waiting for transfers between devices, from_behind(): return lax.ppermute(x, axis, pairs)  39.5 us
    dot_general x8, matrix products, tick_step(): jnp.einsum('hpnjc,hpjd->ncd', grad_events, weight_four, preferred_element...  38.3 us
    dot_general x8, matrix products, head_backward(): jnp.einsum('hnjq,hnkjc->hnqkc', query_act, key_tiles, preferred_element_t...  34.1 us
    all_to_all x8, starting transfers between devices, tick_step(): lax.all_to_all(cot_gate, 'ctx', split_axis=0, concat_axis=1, tiled=True)  33.5 us
    dot_general x8, matrix products, head_backward(): jnp.einsum('hnjq,hnkjc->hnqkc', grad_attended, value_tiles, preferred_ele...  23.4 us
  transfers between devices with their start and end apart: 26, of which 18 were waited for; matrix products, arithmetic and copies ran while one was open for 15% of the time, Pallas kernels for 0%

commit v1 on v0

v1 whole, which is shorter than its diff:
```python
import functools

import jax
import jax.numpy as jnp
from jax import lax
from jax.experimental import pallas as pl
from jax.experimental.pallas import tpu as pltpu
from jax.sharding import PartitionSpec as P

BLOCK = 128
HD = 64
HOPS = 4
MESH = pl.DeviceIdType.MESH
F32 = jnp.float32
BF16 = jnp.bfloat16


def silu_slope(argument):
    sigma = jax.nn.sigmoid(argument)
    return sigma * (1.0 + argument * (1.0 - sigma))


def forward(proj, gain, blocks, ranker):
    count = proj.shape[0]
    scale = HD ** (-0.5)
    pre = proj.reshape(count, 4, HD, BLOCK).astype(F32)
    act = jax.nn.silu(pre).astype(BF16)
    slopes = silu_slope(pre)
    onehot = (blocks[:, :, None] == jnp.arange(count, dtype=jnp.int32)[None, None, :])
    half = onehot.astype(BF16)
    ktile = jnp.einsum("nsm,mjk->njsk", half, act[:, 3], preferred_element_type=F32).astype(BF16)
    vtile = jnp.einsum("nsm,mjk->nskj", half, act[:, 1], preferred_element_type=F32).astype(BF16)
    offsets = jnp.arange(BLOCK, dtype=jnp.int32)
    ranks = ranker.reshape(count, BLOCK).astype(F32)
    key_rank = jnp.einsum("nsm,mk->nsk", onehot.astype(F32), ranks)
    key_pos = blocks[:, :, None] * BLOCK + offsets
    query_pos = jnp.arange(count * BLOCK, dtype=jnp.int32).reshape(count, BLOCK)
    allowed = (
        (blocks >= 0)[:, :, None, None]
        & (key_pos[:, :, :, None] <= query_pos[:, None, None, :])
        & (key_rank[:, :, :, None] == ranks[:, None, None, :])
    )
    query = act[:, 2]
    scores = jnp.einsum("njsk,njq->nskq", ktile, query, preferred_element_type=F32) * scale
    weights = jnp.where(allowed, jax.nn.silu(scores), 0.0).astype(BF16)
    slope = (jnp.where(allowed, silu_slope(scores), 0.0) * scale).astype(BF16)
    attended = jnp.einsum("nskq,nskj->njq", weights, vtile, preferred_element_type=F32)
    inv_rms = lax.rsqrt(jnp.mean(attended * attended, axis=1, keepdims=True) + 1.0)
    normed = attended * inv_rms
    gain_col = gain[None, :, None]
    ahead = inv_rms * gain_col * act[:, 0].astype(F32)
    factors = jnp.stack([gain_col * normed * slopes[:, 0], slopes[:, 2], slopes[:, 1], slopes[:, 3]], axis=1)
    slots = blocks.shape[1]
    return (
        weights.reshape(count, slots * BLOCK, BLOCK),
        slope.reshape(count, slots * BLOCK, BLOCK),
        ktile.reshape(count, HD, slots * BLOCK),
        vtile.reshape(count, slots * BLOCK, HD),
        query,
        ahead,
        normed,
        factors,
    )


def segment_plan(third):
    count = third.shape[0]
    ids = jnp.arange(count, dtype=jnp.int32)
    before = (third[None, :] < third[:, None]) | ((third[None, :] == third[:, None]) & (ids[None, :] < ids[:, None]))
    place = jnp.sum(before.astype(jnp.int32), axis=1)
    order = jnp.sum(jnp.where(place[None, :] == ids[:, None], ids[None, :], 0), axis=1)
    ordered = jnp.sum(jnp.where(place[None, :] == ids[:, None], third[None, :], 0), axis=1)
    keep = (ordered == jnp.concatenate([ordered[:1] - 1, ordered[:-1]])).astype(F32)
    upto = jnp.sum((third[None, :] <= ids[:, None]).astype(jnp.int32), axis=1)
    has = jnp.any(third[None, :] == ids[:, None], axis=1).astype(F32)
    last = jnp.maximum(upto - 1, 0)
    return jnp.stack([order, last]), jnp.stack([keep, has])


def chain_kernel(
    order_ref, keep_ref, up_ref, wo_ref, wi_ref, w_ref, sp_ref, kt_ref, vt_ref, q_ref, ahead_ref, normed_ref, fac_ref,
    sg_ref, gpa_ref, gpb_ref,
    wot, upbuf, sgsend, cotsend, cotin, gain_a, gain_b, gvt, gkt, segv, segk, acc,
    cs, cr, as_, ar, bs, br, hs, hr,
):
    count = w_ref.shape[0]
    s = lax.axis_index("pipe")
    c = lax.axis_index("ctx")
    sections = lax.axis_size("pipe")
    width = up_ref.shape[1]
    cols = width // HOPS
    first = s == sections - 1

    def peer(d):
        return lax.rem(c + d, count)

    def behind(d):
        return lax.rem(c - d + count, count)

    barrier = pltpu.get_barrier_semaphore()
    for d in range(1, count):
        pl.semaphore_signal(barrier, inc=1, device_id=(s, peer(d)), device_id_type=MESH)

    for d in (1, sections - 1):
        pl.semaphore_signal(barrier, inc=1, device_id=(lax.rem(s + d, sections), c), device_id_type=MESH)

    wot[...] = wo_ref[...].T
    pl.semaphore_wait(barrier, count + 1)

    def hop(i):
        return pltpu.make_async_remote_copy(
            src_ref=sgsend.at[i], dst_ref=upbuf.at[i], send_sem=hs.at[i], recv_sem=hr.at[i],
            device_id=(s - 1, c), device_id_type=MESH,
        )

    @pl.when(first)
    def _():
        for i in range(HOPS):
            upbuf[i] = up_ref[:, i * cols : (i + 1) * cols]

    cot = None
    for i in range(HOPS):
        @pl.when(jnp.logical_not(first))
        def _(i=i):
            hop(i).wait_recv()

        part = lax.dot_general(
            wot[:, i * cols : (i + 1) * cols], upbuf[i], (((1,), (1,)), ((), ())), preferred_element_type=F32
        )
        cot = part if cot is None else cot + part
    cotsend[...] = cot.astype(BF16).reshape(count, HD, BLOCK)

    def cot_copy(d):
        h = peer(d)
        return pltpu.make_async_remote_copy(
            src_ref=cotsend.at[h], dst_ref=cotin.at[c], send_sem=cs.at[h], recv_sem=cr.at[c],
            device_id=(s, h), device_id_type=MESH,
        )

    def cot_arrival(n):
        return pltpu.make_async_remote_copy(
            src_ref=cotsend.at[n], dst_ref=cotin.at[n], send_sem=cs.at[n], recv_sem=cr.at[n],
            device_id=(s, n), device_id_type=MESH,
        )

    def start_cot(d, carry):
        cot_copy(d).start()
        return carry

    lax.fori_loop(1, count, start_cot, 0)
    cotin[c] = cotsend[c]

    def back_copy(src, landing, send, recv, n):
        return pltpu.make_async_remote_copy(
            src_ref=src.at[n], dst_ref=landing.at[c], send_sem=send.at[n], recv_sem=recv.at[c],
            device_id=(s, n), device_id_type=MESH,
        )

    def back_arrival(src, landing, send, recv, h):
        return pltpu.make_async_remote_copy(
            src_ref=src.at[h], dst_ref=landing.at[h], send_sem=send.at[h], recv_sem=recv.at[h],
            device_id=(s, h), device_id_type=MESH,
        )

    def head_step(i, carry):
        n = behind(i)

        @pl.when(i > 0)
        def _():
            cot_arrival(n).wait_recv()

        cot_n = cotin[n].astype(F32)
        normed = normed_ref[n]
        steep = cot_n * ahead_ref[n]
        mean = jnp.sum(steep * normed, axis=0, keepdims=True) * (1.0 / HD)
        ga = (steep - normed * mean).astype(BF16)
        gw = jnp.dot(vt_ref[n], ga, preferred_element_type=F32)
        gs = (gw * sp_ref[n].astype(F32)).astype(BF16)
        gq = jnp.dot(kt_ref[n], gs, preferred_element_type=F32)
        gpa_ref[n, :HD] = (cot_n * fac_ref[n, 0]).astype(BF16)
        gpa_ref[n, HD:] = (gq * fac_ref[n, 1]).astype(BF16)

        @pl.when(i > 0)
        def _():
            back_copy(gpa_ref, gain_a, as_, ar, n).start()

        gvt[n] = lax.dot_general(ga, w_ref[n], (((1,), (1,)), ((), ())), preferred_element_type=F32)
        gkt[n] = lax.dot_general(q_ref[n], gs, (((1,), (1,)), ((), ())), preferred_element_type=F32)
        return carry

    lax.fori_loop(0, count, head_step, 0)
    gain_a[c] = gpa_ref[c]

    def seg_step(i, carry):
        run_v, run_k = carry
        n = order_ref[0, i]
        keep = keep_ref[0, i]
        run_v = run_v * keep + gvt[n, :, 2 * BLOCK :]
        run_k = run_k * keep + gkt[n, :, 2 * BLOCK :]
        segv[i] = run_v
        segk[i] = run_k
        return run_v, run_k

    zero = jnp.zeros((HD, BLOCK), F32)
    lax.fori_loop(0, count, seg_step, (zero, zero))

    def final_step(i, carry):
        m = behind(i)
        after = lax.rem(m + 1, count)
        last = order_ref[1, m]
        has = keep_ref[1, m]
        gv = gvt[m, :, :BLOCK] + gvt[after, :, BLOCK : 2 * BLOCK] + segv[last] * has
        gk = gkt[m, :, :BLOCK] + gkt[after, :, BLOCK : 2 * BLOCK] + segk[last] * has
        gpb_ref[m, :HD] = (gv * fac_ref[m, 2]).astype(BF16)
        gpb_ref[m, HD:] = (gk * fac_ref[m, 3]).astype(BF16)

        @pl.when(i > 0)
        def _():
            back_copy(gpb_ref, gain_b, bs, br, m).start()

        return carry

    lax.fori_loop(0, count, final_step, 0)
    gain_b[c] = gpb_ref[c]

    for i in range(HOPS):
        acc[:, i * cols : (i + 1) * cols] = upbuf[i].astype(F32)

    def a_rows(h):
        return jnp.concatenate([wi_ref[h, 0], wi_ref[h, 2]], axis=0)

    def b_rows(h):
        return jnp.concatenate([wi_ref[h, 1], wi_ref[h, 3]], axis=0)

    def tdot(left, right):
        return lax.dot_general(left, right, (((0,), (0,)), ((), ())), preferred_element_type=F32)

    def a_step(i, carry):
        h0 = peer(2 * i)
        h1 = peer(2 * i + 1)

        @pl.when(i > 0)
        def _():
            back_arrival(gpa_ref, gain_a, as_, ar, h0).wait_recv()

        back_arrival(gpa_ref, gain_a, as_, ar, h1).wait_recv()
        left = jnp.concatenate([gain_a[h0], gain_a[h1]], axis=0)
        right = jnp.concatenate([a_rows(h0), a_rows(h1)], axis=0)
        acc[...] += tdot(left, right)
        return carry

    lax.fori_loop(0, count // 2, a_step, 0)

    def b_step(i, carry):
        h0 = peer(2 * i)
        h1 = peer(2 * i + 1)

        @pl.when(i > 0)
        def _():
            back_arrival(gpb_ref, gain_b, bs, br, h0).wait_recv()

        back_arrival(gpb_ref, gain_b, bs, br, h1).wait_recv()
        left = jnp.concatenate([gain_b[h0], gain_b[h1]], axis=0)
        right = jnp.concatenate([b_rows(h0), b_rows(h1)], axis=0)
        acc[...] += tdot(left, right)
        return carry

    lax.fori_loop(0, count // 2 - 1, b_step, 0)
    h0 = peer(count - 2)
    h1 = peer(count - 1)
    back_arrival(gpb_ref, gain_b, bs, br, h0).wait_recv()
    back_arrival(gpb_ref, gain_b, bs, br, h1).wait_recv()
    left = jnp.concatenate([gain_b[h0], gain_b[h1]], axis=0)
    for i in range(HOPS):
        span = slice(i * cols, (i + 1) * cols)
        right = jnp.concatenate(
            [wi_ref[h0, 1, :, span], wi_ref[h0, 3, :, span], wi_ref[h1, 1, :, span], wi_ref[h1, 3, :, span]], axis=0
        )
        part = (acc[:, span] + tdot(left, right)).astype(BF16)
        sgsend[i] = part

        @pl.when(s > 0)
        def _(i=i):
            hop(i).start()

        sg_ref[:, span] = part

    def finish(d, carry):
        h = peer(d)
        cot_copy(d).wait_send()
        back_copy(gpa_ref, gain_a, as_, ar, h).wait_send()
        back_copy(gpb_ref, gain_b, bs, br, h).wait_send()
        return carry

    lax.fori_loop(1, count, finish, 0)

    @pl.when(s > 0)
    def _():
        for i in range(HOPS):
            hop(i).wait_send()


def run_chain(plan, keep, up, wo, wi, fwd):
    count = fwd[0].shape[0]
    width = up.shape[1]
    vmem = pl.BlockSpec(memory_space=pltpu.VMEM)
    smem = pl.BlockSpec(memory_space=pltpu.SMEM)
    dma = pltpu.SemaphoreType.DMA
    slots = fwd[0].shape[1]
    pair = (count, 2 * HD, BLOCK)
    return pl.pallas_call(
        chain_kernel,
        out_shape=(
            jax.ShapeDtypeStruct((BLOCK, width), BF16),
            jax.ShapeDtypeStruct(pair, BF16),
            jax.ShapeDtypeStruct(pair, BF16),
        ),
        in_specs=[smem, smem] + [vmem] * 11,
        out_specs=(vmem, vmem, vmem),
        scratch_shapes=[
            pltpu.VMEM((width, width), BF16),
            pltpu.VMEM((HOPS, BLOCK, width // HOPS), BF16),
            pltpu.VMEM((HOPS, BLOCK, width // HOPS), BF16),
            pltpu.VMEM((count, HD, BLOCK), BF16),
            pltpu.VMEM((count, HD, BLOCK), BF16),
            pltpu.VMEM(pair, BF16),
            pltpu.VMEM(pair, BF16),
            pltpu.VMEM((count, HD, slots), F32),
            pltpu.VMEM((count, HD, slots), F32),
            pltpu.VMEM((count, HD, BLOCK), F32),
            pltpu.VMEM((count, HD, BLOCK), F32),
            pltpu.VMEM((BLOCK, width), F32),
            dma((count,)), dma((count,)), dma((count,)), dma((count,)), dma((count,)), dma((count,)),
            dma((HOPS,)), dma((HOPS,)),
        ],
        compiler_params=pltpu.CompilerParams(
            collective_id=0, has_side_effects=True, vmem_limit_bytes=56 * 1024 * 1024
        ),
        cost_estimate=pl.CostEstimate(flops=4 * 10**9, bytes_accessed=20 * 10**6, transcendentals=0),
    )(plan, keep, up, wo, wi, *fwd)


def per_device(key_blocks, ranker, section_inputs, output_grad, input_proj, output_proj, norm_gain):
    count = lax.axis_size("ctx")
    c = lax.axis_index("ctx")
    x = section_inputs[0, 0]
    width = x.shape[1]
    blocks = key_blocks[0]
    wi = input_proj[0].reshape(count, 4, HD, width)
    gain = lax.dynamic_slice_in_dim(norm_gain[0], c * HD, HD)
    x_all = lax.all_gather(x, "ctx", axis=0, tiled=False)
    proj = jnp.einsum("rd,ned->nre", input_proj[0], x[None], preferred_element_type=F32).astype(BF16)
    proj = proj.reshape(count, 4 * HD, BLOCK)
    proj = lax.all_to_all(proj, "ctx", split_axis=0, concat_axis=0, tiled=True)
    fwd = forward(proj, gain, blocks, ranker[0])
    plan, keep = segment_plan(blocks[:, 2])
    sg, gpa, gpb = run_chain(plan, keep, output_grad[0], output_proj[0], wi, fwd)
    factor = float(count * BLOCK) ** (-0.5)
    wa = jnp.einsum("nre,ned->rd", gpa, x_all, preferred_element_type=F32) * factor
    wb = jnp.einsum("nre,ned->rd", gpb, x_all, preferred_element_type=F32) * factor
    weight = jnp.concatenate([wa[:HD], wb[:HD], wa[HD:], wb[HD:]], axis=0)
    return sg[None, None], weight[None]


def solution(mesh):
    placed = (
        P(),
        P(),
        P("pipe", None, "ctx", None),
        P(None, "ctx", None),
        P("pipe", None, None),
        P("pipe", None, None),
        P("pipe", None),
    )
    return jax.shard_map(
        per_device,
        mesh=mesh,
        in_specs=placed,
        out_specs=(P("pipe", None, "ctx", None), P("pipe", "ctx", None)),
        check_vma=False,
    )
```

time: 691 us -> 275 us (0.40)
  waiting for transfers between devices: 262 us -> 20 us
  Pallas kernels: 0 us -> 196 us
  matrix products: 195 us -> 18.2 us
  starting transfers between devices: 109 us -> 8.17 us
  other arithmetic: 80.2 us -> 8.94 us
  local copies, waits for them, and re-layouts: 24.5 us -> 9.19 us
    pallas_call x0 -> x1, Pallas kernels: none -> 196 us  [run_chain(): pl.pallas_call(chain_kernel, out_shape=(jax.ShapeDtypeStruct((BLOCK, widt...]
    dot_general x98 -> x8, matrix products: 176 us -> 18.2 us  [the longest x1 6.34 us: per_device(): jnp.einsum('rd,ned->nre', input_proj[0], x[None], preferred_element_type=...]
    all_to_all x17 -> x1, waiting for transfers between devices: 122 us -> 19.3 us  [per_device(): proj = lax.all_to_all(proj, 'ctx', split_axis=0, concat_axis=0, tiled=True)]
    reduce_scatter x1 -> x0, waiting for transfers between devices: 100 us -> none  [per_device(): lax.psum_scatter(term.reshape(lax.axis_size('ctx') * row_count, width_all...]
    all_to_all x17 -> x1, starting transfers between devices: 98.5 us -> 8.13 us  [per_device(): proj = lax.all_to_all(proj, 'ctx', split_axis=0, concat_axis=0, tiled=True)]
    convert_element_type x33 -> x1, other arithmetic: 49 us -> 0.01 us  [forward(): ranks = ranker.reshape(count, BLOCK).astype(F32)]
    ppermute x8 -> x0, waiting for transfers between devices: 39.5 us -> none  [from_behind(): return lax.ppermute(x, axis, pairs)]
    while x8 -> x0, matrix products: 19.9 us -> none
  transfers between devices with their start and end apart: 26 -> 2, of which waited for: 18 -> 1; matrix products, arithmetic and copies ran while one was open for 15% -> 10% of each run, Pallas kernels for 0% -> 71%
where the time goes in v1:
time: 275 us
  Pallas kernels  196 us (71%)
  waiting for transfers between devices  20 us (7%)
  matrix products  18.2 us (7%)
  between operations  14.3 us (5%)
  local copies, waits for them, and re-layouts  9.19 us (3%)
  other arithmetic  8.94 us (3%)
  starting transfers between devices  8.17 us (3%)
    pallas_call x1, Pallas kernels, run_chain(): pl.pallas_call(chain_kernel, out_shape=(jax.ShapeDtypeStruct((BLOCK, widt...  196 us
    all_to_all x1, waiting for transfers between devices, per_device(): proj = lax.all_to_all(proj, 'ctx', split_axis=0, concat_axis=0, tiled=True)  19.3 us
    all_to_all x1, starting transfers between devices, per_device(): proj = lax.all_to_all(proj, 'ctx', split_axis=0, concat_axis=0, tiled=True)  8.13 us
    dot_general x1, matrix products, per_device(): jnp.einsum('rd,ned->nre', input_proj[0], x[None], preferred_element_type=...  6.34 us
  transfers between devices with their start and end apart: 2, of which 1 were waited for; matrix products, arithmetic and copies ran while one was open for 10% of the time, Pallas kernels for 71%

profile of v1, /device:TPU:0, one launch (start us, length us, event | category | flops | bytes accessed | tf_op | source)
XLA Modules:
  0.0 275.1 jit_solution(17445031621876720792)
XLA Ops:
  7.2 0.7 all-gather.3.cloned.1.call-update
  7.9 6.3 %fusion.5 = bf16[1,4096,128]{1,2,0:T(8,128)(2,1)S(1)} fusion(bf16[1,4096,1024]{2,1,0:T(8,128)(2,1)} %param.11, bf16[1,1,128,1024]{3,2,1,0:T(8,128)(2,1)} %param.9), kind=kOutput, calls=%fused_computation.3 | convolution fusion | flops 1074266112 | bytes 9699328 | tf_op jit(solution)/shard_map/rd,ned->nre/dot_general | solution.py:352
  14.3 1.3 copy.75
  15.6 8.1 %all-to-all-start = ((bf16[16,256,128]{2,1,0:T(8,128)(2,1)}), bf16[16,256,128]{2,1,0:T(8,128)(2,1)S(1)}, u32[]{:S(2)}, u32[]{:S(2)}) async-start(bf16[16,256,128]{2,1,0:T(8,128)(2,1)} %bitcast.16), calls=%async_computation | async-start | bytes 2097152 | tf_op jit(solution)/shard_map/all_to_all | solution.py:354
  23.8 0.2 fusion.36
  24.2 0.2 convert_reduce_fusion.1
  24.4 0.1 select_reduce_fusion
  24.6 0.5 pad_add_fusion.order_ref
  25.1 0.1 fusion.44
  25.4 0.6 add_convert_fusion.keep_ref
  26.1 19.3 %all-to-all-done = bf16[16,256,128]{2,1,0:T(8,128)(2,1)S(1)} async-done(((bf16[16,256,128]{2,1,0:T(8,128)(2,1)}), bf16[16,256,128]{2,1,0:T(8,128)(2,1)S(1)}, u32[]{:S(2)}, u32[]{:S(2)}) %all-to-all-start) | async-done | bytes 1048608 | tf_op jit(solution)/shard_map/all_to_all | solution.py:354
  45.4 3.0 %add_divide_fusion.1 = (f32[16,4,64,128]{3,2,0,1:T(8,128)}, f32[16,4,64,128]{3,2,0,1:T(8,128)}, bf16[16,4,64,128]{3,2,0,1:T(8,128)(2,1)S(1)}) fusion(bf16[16,4,64,128]{3,2,1,0:T(8,128)(2,1)S(1)} %bitcast.122), kind=kLoop, calls=%fused_computation.16 | loop fusion | flops 4718592 | bytes 6291456 | tf_op jit(solution)/shard_map/jit(silu)/div | solution.py:27
  48.4 0.8 slice_bitcast_fusion.4
  49.1 0.4 fusion.12
  49.5 0.5 copy.63
  50.0 1.4 reshape.145.kt_ref
  51.5 1.4 fusion.13
  52.8 1.8 copy.65
  54.7 5.3 %multiply_convert_fusion = (bf16[16,3,128,128]{3,2,1,0:T(8,128)(2,1)}, bf16[16,3,128,128]{3,2,1,0:T(8,128)(2,1)S(1)}) fusion(f32[16,128]{1,0:T(8,128)S(1)} %bitcast.132, f32[16,3,128]{2,1,0:T(4,128)S(1)} %copy.57, s32[16,128]{1,0:T(8,128)S(1)} %multiply_add_fusion.1, s32[16,3,128]{2,1,0:T(4,128)S(1)} %iota_add_fusion, pred[16,3]{1,0:T(8,128)(4,1)S(1)} %copy.55, ...), kind=kOutput, calls=%fused_computation.8 | convolution fusion | flops 114819072 | bytes 4278272 | tf_op jit(solution)/shard_map/njsk,njq->nskq/dot_general | solution.py:44
  60.0 0.6 multiply_reduce_fusion
  60.7 1.6 copy-done.3
  62.3 0.5 copy_multiply_fusion
  62.8 1.1 fusion.29
  63.9 0.2 fusion.45
  64.1 1.5 pad_maximum_fusion.fac_ref
  65.6 196.3 %shard_map.86 = (bf16[128,1024]{1,0:T(8,128)(2,1)}, bf16[16,128,128]{2,1,0:T(8,128)(2,1)}, bf16[16,128,128]{2,1,0:T(8,128)(2,1)}) custom-call(s32[2,16]{1,0:T(2,128)} %pad_add_fusion.order_ref, f32[2,16]{1,0:T(2,128)} %add_convert_fusion.keep_ref, bf16[128,1024]{1,0:T(8,128)(2,1)} %bitcast.125, bf16[1024,1024]{1,0:T(8,128)(2,1)} %bitcast.123, ...), custom_call_target="tpu_custom_call" | custom-call | flops 4000000000 | bytes 20000000 | tf_op jit(solution)/shard_map/pallas_call | solution.py:311
  261.9 3.2 %fusion.23 = f32[128,1024]{1,0:T(8,128)S(1)} fusion(bf16[16,128,128]{2,1,0:T(8,128)(2,1)} %get-tuple-element.6, bf16[16,1,128,1024]{3,2,1,0:T(8,128)(2,1)} %all-gather.3.cloned.1.call-done), kind=kOutput, calls=%fused_computation.25 | convolution fusion | flops 537001984 | bytes 5242880 | tf_op jit(solution)/shard_map/nre,ned->rd/dot_general | solution.py:359
  265.1 0.4 copy-done.1
  265.5 0.1 copy-done.6
  265.6 0.7 fusion.20
  266.5 1.1 maximum_bitcast_fusion
  267.5 0.7 copy.105
  (35 shorter events, 0.7 us)
Async XLA Ops:
  7.2 18.1 %copy-start = (f32[1,1024]{1,0:T(1,128)S(1)}, f32[1,1024]{1,0:T(1,128)}, u32[]{:S(2)}) copy-start(f32[1,1024]{1,0:T(1,128)} %param.13) | copy-start | bytes 12292
  7.2 254.7 %all-gather.3.cloned.1.call-start = ((), (), s32[]{:S(2)}) async-start(), calls=%async_computation.1 | async-start | bytes 4456448 | tf_op jit(solution)/shard_map/all_gather | solution.py:351
  14.3 9.5 %copy-start.8 = (s32[1,16,3]{1,0,2:T(1,128)S(1)}, s32[1,16,3]{1,0,2:T(1,128)}, u32[]{:S(2)}) copy-start(s32[1,16,3]{1,0,2:T(1,128)} %param.7) | copy-start | bytes 580
  14.3 9.5 %copy-start.9 = (s32[1,2048]{1,0:T(1,128)S(1)}, s32[1,2048]{1,0:T(1,128)}, u32[]{:S(2)}) copy-start(s32[1,2048]{1,0:T(1,128)} %param.8) | copy-start | bytes 24580
  15.6 29.8 %all-to-all-start = ((bf16[16,256,128]{2,1,0:T(8,128)(2,1)}), bf16[16,256,128]{2,1,0:T(8,128)(2,1)S(1)}, u32[]{:S(2)}, u32[]{:S(2)}) async-start(bf16[16,256,128]{2,1,0:T(8,128)(2,1)} %bitcast.16), calls=%async_computation | async-start | bytes 2097152 | tf_op jit(solution)/shard_map/all_to_all | solution.py:354
  54.7 5.4 %copy-start.2 = (bf16[16,3,128,64]{3,2,1,0:T(8,128)(2,1)}, bf16[16,3,128,64]{3,2,1,0:T(8,128)(2,1)S(1)}, u32[]{:S(2)}) copy-start(bf16[16,3,128,64]{3,2,1,0:T(8,128)(2,1)S(1)} %copy.65) | copy-start | bytes 2359300
  54.7 6.0 %copy-start.4 = (f32[16,4,64,128]{3,2,0,1:T(8,128)S(1)}, f32[16,4,64,128]{3,2,0,1:T(8,128)}, u32[]{:S(2)}) copy-start(f32[16,4,64,128]{3,2,0,1:T(8,128)} %get-tuple-element.19) | copy-start | bytes 6291460
  60.0 2.8 %copy-start.5 = (bf16[16,3,128,128]{3,2,1,0:T(8,128)(2,1)}, bf16[16,3,128,128]{3,2,1,0:T(8,128)(2,1)S(1)}, u32[]{:S(2)}) copy-start(bf16[16,3,128,128]{3,2,1,0:T(8,128)(2,1)S(1)} %get-tuple-element.14) | copy-start | bytes 4718596
  60.0 2.2 copy-start.3
  261.9 3.6 %copy-start.1 = (bf16[16,1,128,1024]{3,2,1,0:T(8,128)(2,1)S(1)}, bf16[16,1,128,1024]{3,2,1,0:T(8,128)(2,1)}, u32[]{:S(2)}) copy-start(bf16[16,1,128,1024]{3,2,1,0:T(8,128)(2,1)} %all-gather.3.cloned.1.call-done) | copy-start | bytes 12582916
  261.9 3.7 %copy-start.6 = (bf16[16,128,128]{2,1,0:T(8,128)(2,1)S(1)}, bf16[16,128,128]{2,1,0:T(8,128)(2,1)}, u32[]{:S(2)}) copy-start(bf16[16,128,128]{2,1,0:T(8,128)(2,1)} %get-tuple-element.7) | copy-start | bytes 1572868
  266.3 1.2 copy-start.7
Sparse Core Ops, SparseCore 0:
  10.2 62.9 all-gather.2

commit v2 on v0

v2 whole, which is shorter than its diff:
```python
import math

import jax
import jax.numpy as jnp
from jax import lax
from jax.experimental import pallas as pl
from jax.experimental.pallas import tpu as pltpu
from jax.sharding import PartitionSpec as P

BLOCK = 128
HD = 64
CHUNKS = 4
LATE = 3
MESH = pl.DeviceIdType.MESH
F32 = jnp.float32
BF16 = jnp.bfloat16


def segment_plan(third):
    count = third.shape[0]
    ids = jnp.arange(count, dtype=jnp.int32)
    before = (third[None, :] < third[:, None]) | ((third[None, :] == third[:, None]) & (ids[None, :] < ids[:, None]))
    place = jnp.sum(before.astype(jnp.int32), axis=1)
    order = jnp.sum(jnp.where(place[None, :] == ids[:, None], ids[None, :], 0), axis=1)
    ordered = jnp.sum(jnp.where(place[None, :] == ids[:, None], third[None, :], 0), axis=1)
    keep = (ordered == jnp.concatenate([ordered[:1] - 1, ordered[:-1]])).astype(F32)
    upto = jnp.sum((third[None, :] <= ids[:, None]).astype(jnp.int32), axis=1)
    has = jnp.any(third[None, :] == ids[:, None], axis=1).astype(F32)
    last = jnp.maximum(upto - 1, 0)
    return jnp.stack([order, last]), jnp.stack([keep, has])


def dot(left, right):
    return jnp.dot(left, right, preferred_element_type=F32)


def ntdot(left, right):
    return lax.dot_general(left, right, (((1,), (1,)), ((), ())), preferred_element_type=F32)


def tdot(left, right):
    return lax.dot_general(left, right, (((0,), (0,)), ((), ())), preferred_element_type=F32)


def kernel(
    blocks_ref, order_ref, keep_ref, up_ref, gain_ref, row_ref, col_ref, x_ref, wi_ref, wo_ref,
    sg_ref, dw_ref,
    xv, xt, wi, wo_own, wo_next, psend, pin, xall, gate, query, key, value, keyt, valuet, weight, slope,
    ahead, normed, fac, upbuf, sgsend, cotfirst, cotsend, cotin, gpa, gpb, gain_a, gain_b, gvt, gkt, segv, segk, acc,
    xl, wil, wol, ps, pr, fs, cs, cr, as_, ar, bs, br, xs, xr, us, ur, ws, wr,
):
    count, _, width = xall.shape
    side = math.isqrt(count)
    per_chunk = count // CHUNKS
    s = lax.axis_index("pipe")
    c = lax.axis_index("ctx")
    sections = lax.axis_size("pipe")
    first = s == sections - 1
    cy, cz = c // side, lax.rem(c, side)

    def to(d):
        return lax.rem(cy + d // side, side) * side + lax.rem(cz + d % side, side)

    def source(d):
        return lax.rem(cy + side - d // side, side) * side + lax.rem(cz + side - d % side, side)

    def distance(d):
        y, z = d // side, d % side
        return min(y, side - y) + min(z, side - z)

    near = sorted(range(count), key=distance)
    far = [d for d in near[::-1] if d]

    def remote(src, dst, send, recv, where):
        return pltpu.make_async_remote_copy(
            src_ref=src, dst_ref=dst, send_sem=send, recv_sem=recv, device_id=where, device_id_type=MESH
        )

    x_load = pltpu.make_async_copy(x_ref, xv, xl)
    wo_load = pltpu.make_async_copy(wo_ref, wo_own, wol)

    def wi_load(k):
        span = pl.ds(k * per_chunk, per_chunk)
        return pltpu.make_async_copy(wi_ref.at[span], wi.at[span], wil.at[k])

    def chunk_at(i):
        return lax.rem(c // per_chunk + i, CHUNKS)

    x_load.start()

    @pl.when(first)
    def _():
        wo_load.start()

    for i in range(CHUNKS):
        wi_load(chunk_at(i)).start()

    barrier = pltpu.get_barrier_semaphore()
    after, before = lax.rem(s + 1, sections), lax.rem(s + sections - 1, sections)
    pl.semaphore_signal(barrier, inc=1, device_id=(before, c), device_id_type=MESH)
    for d in range(1, count):
        pl.semaphore_signal(barrier, inc=1, device_id=(s, to(d)), device_id_type=MESH)
    for h in range(count):
        pl.semaphore_signal(barrier, inc=1, device_id=(after, h), device_id_type=MESH)
    pl.semaphore_wait(barrier, 2 * count)

    wo_push = remote(wo_ref, wo_next, ws, wr, (after, c))

    @pl.when(jnp.logical_not(first))
    def _():
        wo_push.start()

    def first_copy(d):
        h = to(d)
        return remote(cotfirst.at[h], cotin.at[c], fs.at[d], cr.at[d], (s, h))

    def cot_copy(d):
        h = to(d)
        return remote(cotsend.at[h], cotin.at[c], cs.at[d], cr.at[d], (before, h))

    def cot_arrival(d):
        n = source(d)
        return remote(cotsend.at[n], cotin.at[n], cs.at[d], cr.at[d], (s, n))

    def set_cot(held, cot):
        held[...] = cot.T.astype(BF16).reshape(count, HD, BLOCK)

    @pl.when(first)
    def _():
        wo_load.wait()
        set_cot(cotfirst, dot(up_ref[...], wo_own[...]))
        for d in far:
            first_copy(d).start()
        cotin[c] = cotfirst[c]
        upbuf[...] = up_ref[...]

    def p_copy(h):
        return remote(psend.at[h], pin.at[c], ps.at[h], pr.at[c], (s, h))

    def p_arrival(h):
        return remote(psend.at[h], pin.at[h], ps.at[h], pr.at[h], (s, h))

    x_load.wait()
    xt[...] = xv[...].T

    def project(i, carry):
        k = chunk_at(i)
        span = pl.ds(k * per_chunk, per_chunk)
        wi_load(k).wait()
        rows = wi[span].reshape(per_chunk * 4 * HD, width)
        psend[span] = dot(rows, xt[...]).astype(BF16).reshape(per_chunk, 4 * HD, BLOCK)
        for j in range(per_chunk):
            h = k * per_chunk + j

            @pl.when(h != c)
            def _(h=h):
                p_copy(h).start()

        return carry

    lax.fori_loop(0, CHUNKS, project, 0)
    pin[c] = psend[c]

    def x_copy(d):
        h = to(d)
        return remote(xv, xall.at[c], xs.at[d], xr.at[d], (s, h))

    def x_arrival(d):
        n = source(d)
        return remote(xv, xall.at[n], xs.at[d], xr.at[d], (s, n))

    def activate(d):
        n = source(d)
        if d:
            p_arrival(n).wait_recv()
        pre = pin[n].astype(F32)
        sigma = jax.nn.sigmoid(pre)
        act = (pre * sigma).astype(BF16)
        slopes = sigma * (1.0 + pre * (1.0 - sigma))
        gate[n] = act[:HD]
        value[n] = act[HD : 2 * HD]
        query[n] = act[2 * HD : 3 * HD]
        key[n] = act[3 * HD :]
        valuet[n] = act[HD : 2 * HD].astype(F32).T.astype(BF16)
        keyt[n] = act[3 * HD :].astype(F32).T.astype(BF16)
        fac[n, 0] = slopes[:HD]
        fac[n, 1] = slopes[2 * HD : 3 * HD]
        fac[n, 2] = slopes[HD : 2 * HD]
        fac[n, 3] = slopes[3 * HD :]

    for d in near:
        activate(d)

    @pl.when(s < LATE)
    def _():
        for d in far:
            x_copy(d).start()

    xall[c] = xv[...]
    scale = HD ** (-0.5)
    gain = gain_ref[...]
    apart = lax.broadcasted_iota(jnp.int32, (BLOCK, BLOCK), 0) - lax.broadcasted_iota(jnp.int32, (BLOCK, BLOCK), 1)

    def slots(n):
        return [blocks_ref[n, t] for t in range(3)]

    def attend(n, carry):
        listed = slots(n)
        at = [jnp.maximum(b, 0) for b in listed]
        scores = dot(jnp.concatenate([keyt[m] for m in at], axis=0), query[n]) * scale
        rank = row_ref[n]
        allowed = jnp.concatenate(
            [
                (apart <= (n - b) * BLOCK) & (col_ref[m] == jnp.where(b >= 0, rank, -1.0))
                for b, m in zip(listed, at)
            ],
            axis=0,
        )
        sigma = jax.nn.sigmoid(scores)
        now = jnp.where(allowed, scores * sigma, 0.0).astype(BF16)
        weight[n] = now
        slope[n] = (jnp.where(allowed, sigma * (1.0 + scores * (1.0 - sigma)), 0.0) * scale).astype(BF16)
        attended = dot(jnp.concatenate([value[m] for m in at], axis=1), now)
        inv_rms = lax.rsqrt(jnp.sum(attended * attended, axis=0, keepdims=True) * (1.0 / HD) + 1.0)
        norm = attended * inv_rms
        normed[n] = norm
        ahead[n] = inv_rms * gain * gate[n].astype(F32)
        fac[n, 0] = gain * norm * fac[n, 0]
        return carry

    lax.fori_loop(0, count, attend, 0, unroll=2)

    def back_copy(src, landing, send, recv, d):
        n = source(d)
        return remote(src.at[n], landing.at[c], send.at[d], recv.at[d], (s, n))

    def back_arrival(src, landing, send, recv, d):
        h = to(d)
        return remote(src.at[h], landing.at[h], send.at[d], recv.at[d], (s, h))

    def head(d):
        n = source(d)
        at = [jnp.maximum(b, 0) for b in slots(n)]
        cot_n = cotin[n].astype(F32)
        norm = normed[n]
        steep = cot_n * ahead[n]
        mean = jnp.sum(steep * norm, axis=0, keepdims=True) * (1.0 / HD)
        ga = (steep - norm * mean).astype(BF16)
        gw = dot(jnp.concatenate([valuet[m] for m in at], axis=0), ga)
        gs = (gw * slope[n].astype(F32)).astype(BF16)
        gq = dot(jnp.concatenate([key[m] for m in at], axis=1), gs)
        gpa[n, :HD] = (cot_n * fac[n, 0]).astype(BF16)
        gpa[n, HD:] = (gq * fac[n, 1]).astype(BF16)
        gvt[n] = ntdot(ga, weight[n])
        gkt[n] = ntdot(query[n], gs)

    group = 4
    for g in range(0, count, group):
        for d in near[g : g + group]:
            if d:
                cot_arrival(d).wait_recv()
            else:

                @pl.when(jnp.logical_not(first))
                def _(d=d):
                    cot_arrival(d).wait_recv()

        for d in near[g : g + group]:
            head(d)
        for d in near[g : g + group]:
            if d:
                back_copy(gpa, gain_a, as_, ar, d).start()
    gain_a[c] = gpa[c]

    def seg_step(i, carry):
        run_v, run_k = carry
        n = order_ref[0, i]
        keep = keep_ref[0, i]
        run_v = run_v * keep + gvt[n, :, 2 * BLOCK :]
        run_k = run_k * keep + gkt[n, :, 2 * BLOCK :]
        segv[i] = run_v
        segk[i] = run_k
        return run_v, run_k

    zero = jnp.zeros((HD, BLOCK), F32)
    lax.fori_loop(0, count, seg_step, (zero, zero), unroll=2)

    def finalise(d):
        m = source(d)
        later = lax.rem(m + 1, count)
        last = order_ref[1, m]
        has = keep_ref[1, m]
        gv = gvt[m, :, :BLOCK] + gvt[later, :, BLOCK : 2 * BLOCK] + segv[last] * has
        gk = gkt[m, :, :BLOCK] + gkt[later, :, BLOCK : 2 * BLOCK] + segk[last] * has
        gpb[m, :HD] = (gv * fac[m, 2]).astype(BF16)
        gpb[m, HD:] = (gk * fac[m, 3]).astype(BF16)

    for d in far:
        finalise(d)
        back_copy(gpb, gain_b, bs, br, d).start()
    finalise(0)
    gain_b[c] = gpb[c]

    norm_factor = float(count * BLOCK) ** (-0.5)

    def weight_grad():
        for d in far[::-1]:
            x_arrival(d).wait_recv()
        whole = xall[...].reshape(count * BLOCK, width)
        for src, base in ((gpa, 0), (gpb, HD)):
            part = dot(jnp.concatenate([src[n] for n in range(count)], axis=1), whole) * norm_factor
            dw_ref[base : base + HD] = part[:HD]
            dw_ref[base + 2 * HD : base + 3 * HD] = part[HD:]

    def half_weights(parts, span):
        return jnp.concatenate([wi[h, p, :, span] for h in range(count) for p in parts], axis=0)

    for d in near[1:]:
        back_arrival(gpa, gain_a, as_, ar, d).wait_recv()
    left = gain_a[...].reshape(count * BLOCK, BLOCK)

    @pl.when(jnp.logical_not(first))
    def _():
        remote(sgsend, upbuf, us, ur, (s, c)).wait_recv()
        wo_push.wait_send()
    acc[...] = upbuf[...].astype(F32) + tdot(left, half_weights((0, 2), slice(None)))

    @pl.when(s < LATE)
    def _():
        weight_grad()

    @pl.when(s > 0)
    def _():
        remote(wo_ref, wo_next, ws, wr, (s, c)).wait_recv()

    for d in near[1:]:
        back_arrival(gpb, gain_b, bs, br, d).wait_recv()
    left = gain_b[...].reshape(count * BLOCK, BLOCK)
    cols = width // CHUNKS
    for i in range(CHUNKS):
        span = slice(i * cols, (i + 1) * cols)
        part = (acc[:, span] + tdot(left, half_weights((1, 3), span))).astype(BF16)
        sgsend[:, span] = part
        sg_ref[:, span] = part

    up_push = remote(sgsend, upbuf, us, ur, (before, c))

    @pl.when(s > 0)
    def _():
        set_cot(cotsend, dot(sgsend[...], wo_next[...]))
        for d in far + [0]:
            cot_copy(d).start()
        up_push.start()

    @pl.when(s >= LATE)
    def _():
        for d in far:
            x_copy(d).start()
        weight_grad()

    @pl.when(first)
    def _():
        for d in far:
            first_copy(d).wait_send()

    for d in far:
        p_copy(to(d)).wait_send()
        back_copy(gpa, gain_a, as_, ar, d).wait_send()
        back_copy(gpb, gain_b, bs, br, d).wait_send()
        x_copy(d).wait_send()

    @pl.when(s > 0)
    def _():
        for d in far + [0]:
            cot_copy(d).wait_send()
        up_push.wait_send()


def per_device(key_blocks, ranker, section_inputs, output_grad, input_proj, output_proj, norm_gain):
    count = lax.axis_size("ctx")
    c = lax.axis_index("ctx")
    x = section_inputs[0, 0]
    width = x.shape[1]
    blocks = key_blocks[0]
    gain = lax.dynamic_slice_in_dim(norm_gain[0], c * HD, HD)
    gain = jnp.broadcast_to(gain[:, None], (HD, BLOCK))
    ranks = ranker[0].reshape(count, BLOCK).astype(F32)
    order, keep = segment_plan(blocks[:, 2])
    vmem = pl.BlockSpec(memory_space=pltpu.VMEM)
    smem = pl.BlockSpec(memory_space=pltpu.SMEM)
    hbm = pl.BlockSpec(memory_space=pl.ANY)
    dma = pltpu.SemaphoreType.DMA
    full = 3 * BLOCK

    def half(*shape):
        return pltpu.VMEM(shape, BF16)

    def single(*shape):
        return pltpu.VMEM(shape, F32)

    sg, dw = pl.pallas_call(
        kernel,
        out_shape=(
            jax.ShapeDtypeStruct((BLOCK, width), BF16),
            jax.ShapeDtypeStruct((4 * HD, width), F32),
        ),
        in_specs=[smem, smem, smem, vmem, vmem, vmem, vmem, hbm, hbm, hbm],
        out_specs=(vmem, vmem),
        scratch_shapes=[
            half(BLOCK, width),
            half(width, BLOCK),
            half(count, 4, HD, width),
            half(width, width),
            half(width, width),
            half(count, 4 * HD, BLOCK),
            half(count, 4 * HD, BLOCK),
            half(count, BLOCK, width),
            half(count, HD, BLOCK),
            half(count, HD, BLOCK),
            half(count, HD, BLOCK),
            half(count, HD, BLOCK),
            half(count, BLOCK, HD),
            half(count, BLOCK, HD),
            half(count, full, BLOCK),
            half(count, full, BLOCK),
            single(count, HD, BLOCK),
            single(count, HD, BLOCK),
            single(count, 4, HD, BLOCK),
            half(BLOCK, width),
            half(BLOCK, width),
            half(count, HD, BLOCK),
            half(count, HD, BLOCK),
            half(count, HD, BLOCK),
            half(count, 2 * HD, BLOCK),
            half(count, 2 * HD, BLOCK),
            half(count, 2 * HD, BLOCK),
            half(count, 2 * HD, BLOCK),
            single(count, HD, full),
            single(count, HD, full),
            single(count, HD, BLOCK),
            single(count, HD, BLOCK),
            single(BLOCK, width),
            dma,
            dma((CHUNKS,)),
            dma,
        ]
        + [dma((count,)) for _ in range(11)]
        + [dma for _ in range(4)],
        compiler_params=pltpu.CompilerParams(
            collective_id=0, has_side_effects=True, vmem_limit_bytes=58 * 1024 * 1024
        ),
        cost_estimate=pl.CostEstimate(flops=5 * 10**9, bytes_accessed=20 * 10**6, transcendentals=0),
    )(
        blocks, order, keep, output_grad[0], gain, ranks[:, None, :], ranks[:, :, None],
        x, input_proj[0].reshape(count, 4, HD, width), output_proj[0],
    )
    return sg[None, None], dw[None]


def solution(mesh):
    placed = (
        P(),
        P(),
        P("pipe", None, "ctx", None),
        P(None, "ctx", None),
        P("pipe", None, None),
        P("pipe", None, None),
        P("pipe", None),
    )
    return jax.shard_map(
        per_device,
        mesh=mesh,
        in_specs=placed,
        out_specs=(P("pipe", None, "ctx", None), P("pipe", "ctx", None)),
        check_vma=False,
    )
```

time: 691 us -> 229 us (0.33)
  waiting for transfers between devices: 262 us -> 0 us
  Pallas kernels: 0 us -> 217 us
  matrix products: 195 us -> 0 us
  starting transfers between devices: 109 us -> 0 us
  other arithmetic: 80.2 us -> 3.01 us
  local copies, waits for them, and re-layouts: 24.5 us -> 8.13 us
  between operations: 14.1 us -> 0.72 us
    pallas_call x0 -> x1, Pallas kernels: none -> 217 us  [per_device(): pl.pallas_call(kernel, out_shape=(jax.ShapeDtypeStruct((BLOCK, width), BF...]
    dot_general x98 -> x0, matrix products: 176 us -> none  [the longest x8 38.3 us: tick_step(): jnp.einsum('hpnjc,hpjd->ncd', grad_events, weight_four, preferred_element...]
    all_to_all x17 -> x0, waiting for transfers between devices: 122 us -> none  [the longest x8 108 us: tick_step(): lax.all_to_all(grad_heads, 'ctx', split_axis=2, concat_axis=0, tiled=True)]
    reduce_scatter x1 -> x0, waiting for transfers between devices: 100 us -> none  [per_device(): lax.psum_scatter(term.reshape(lax.axis_size('ctx') * row_count, width_all...]
    all_to_all x17 -> x0, starting transfers between devices: 98.5 us -> none  [the longest x8 56.7 us: tick_step(): lax.all_to_all(grad_heads, 'ctx', split_axis=2, concat_axis=0, tiled=True)]
    convert_element_type x33 -> x1, other arithmetic: 49 us -> 1.3 us  [per_device(): ranks = ranker[0].reshape(count, BLOCK).astype(F32)]
    ppermute x8 -> x0, waiting for transfers between devices: 39.5 us -> none  [from_behind(): return lax.ppermute(x, axis, pairs)]
    while x8 -> x0, matrix products: 19.9 us -> none
  transfers between devices with their start and end apart: 26 -> 0, of which waited for: 18 -> 0; matrix products, arithmetic and copies ran while one was open for 15% -> 0% of each run, Pallas kernels for 0% -> 0%
where the time goes in v2:
time: 229 us
  Pallas kernels  217 us (95%)
  local copies, waits for them, and re-layouts  8.13 us (4%)
  other arithmetic  3.01 us (1%)
    pallas_call x1, Pallas kernels, per_device(): pl.pallas_call(kernel, out_shape=(jax.ShapeDtypeStruct((BLOCK, width), BF...  217 us
    unnamed x5, local copies, waits for them, and re-layouts  5.34 us

profile of v2, /device:TPU:0, one launch (start us, length us, event | category | flops | bytes accessed | tf_op | source)
XLA Modules:
  0.0 229.2 jit_solution(17741449893395371089)
XLA Ops:
  0.6 0.0 copy-start
  0.6 0.7 copy-done
  1.3 0.1 dynamic-slice_bitcast_fusion
  1.4 0.7 copy.16
  2.1 0.2 convert_reduce_fusion.1
  2.3 0.1 fusion.2
  2.4 0.1 select_reduce_fusion
  2.6 0.6 pad_add_fusion.order_ref
  3.2 0.1 add_compare_fusion
  3.3 0.6 add_convert_fusion.keep_ref
  3.9 0.7 copy.12.blocks_ref
  4.5 1.3 fusion.3
  5.8 0.7 broadcast_in_dim.24.gain_ref
  6.5 1.3 copy.13.col_ref
  7.9 217.3 %shard_map.86 = (bf16[128,1024]{1,0:T(8,128)(2,1)}, f32[256,1024]{1,0:T(8,128)}) custom-call(s32[16,3]{1,0:T(8,128)} %copy.12.blocks_ref, s32[2,16]{1,0:T(2,128)} %pad_add_fusion.order_ref, f32[2,16]{1,0:T(2,128)} %add_convert_fusion.keep_ref, bf16[128,1024]{1,0:T(8,128)(2,1)} %bitcast.36, f32[64,128]{1,0:T(8,128)} %broadcast_in_dim.24.gain_ref, ...), custom_call_target="tpu_custom_call" | custom-call | flops 5000000000 | bytes 20000000 | tf_op jit(solution)/shard_map/pallas_call | solution.py:401
  225.2 1.7 copy.19
  226.8 2.3 %copy.20 = f32[1,256,1024]{2,1,0:T(8,128)} copy(f32[1,256,1024]{2,1,0:T(8,128)} %bitcast.26) | data formatting | bytes 2097152
  (3 shorter events, 0.0 us)
Async XLA Ops:
  0.6 0.7 copy-start

commit v3 on v2

--- a/solution.py
+++ b/solution.py
@@ -10,7 +10,6 @@
 BLOCK = 128
 HD = 64
 CHUNKS = 4
-LATE = 3
 MESH = pl.DeviceIdType.MESH
 F32 = jnp.float32
 BF16 = jnp.bfloat16
@@ -47,7 +46,7 @@
     sg_ref, dw_ref,
     xv, xt, wi, wo_own, wo_next, psend, pin, xall, gate, query, key, value, keyt, valuet, weight, slope,
     ahead, normed, fac, upbuf, sgsend, cotfirst, cotsend, cotin, gpa, gpb, gain_a, gain_b, gvt, gkt, segv, segk, acc,
-    xl, wil, wol, ps, pr, fs, cs, cr, as_, ar, bs, br, xs, xr, us, ur, ws, wr,
+    xl, wil, wol, ps, pr, fs, cs, cr, as_, ar, bs, br, xs, xr, us, ur, ws, wr, go,
 ):
     count, _, width = xall.shape
     side = math.isqrt(count)
@@ -56,6 +55,8 @@
     c = lax.axis_index("ctx")
     sections = lax.axis_size("pipe")
     first = s == sections - 1
+    second = s == sections - 2
+    late = first | second | (s == sections - 4)
     cy, cz = c // side, lax.rem(c, side)
 
     def to(d):
@@ -125,15 +126,6 @@
     def set_cot(held, cot):
         held[...] = cot.T.astype(BF16).reshape(count, HD, BLOCK)
 
-    @pl.when(first)
-    def _():
-        wo_load.wait()
-        set_cot(cotfirst, dot(up_ref[...], wo_own[...]))
-        for d in far:
-            first_copy(d).start()
-        cotin[c] = cotfirst[c]
-        upbuf[...] = up_ref[...]
-
     def p_copy(h):
         return remote(psend.at[h], pin.at[c], ps.at[h], pr.at[c], (s, h))
 
@@ -158,8 +150,21 @@
 
         return carry
 
+    @pl.when(second)
+    def _():
+        pl.semaphore_wait(go, 1)
+
     lax.fori_loop(0, CHUNKS, project, 0)
     pin[c] = psend[c]
+
+    @pl.when(first)
+    def _():
+        wo_load.wait()
+        set_cot(cotfirst, dot(up_ref[...], wo_own[...]))
+        for d in far:
+            first_copy(d).start()
+        cotin[c] = cotfirst[c]
+        upbuf[...] = up_ref[...]
 
     def x_copy(d):
         h = to(d)
@@ -191,7 +196,11 @@
     for d in near:
         activate(d)
 
-    @pl.when(s < LATE)
+    @pl.when(first)
+    def _():
+        pl.semaphore_signal(go, inc=1, device_id=(before, c), device_id_type=MESH)
+
+    @pl.when(jnp.logical_not(late))
     def _():
         for d in far:
             x_copy(d).start()
@@ -325,7 +334,7 @@
         wo_push.wait_send()
     acc[...] = upbuf[...].astype(F32) + tdot(left, half_weights((0, 2), slice(None)))
 
-    @pl.when(s < LATE)
+    @pl.when(jnp.logical_not(late))
     def _():
         weight_grad()
 
@@ -352,7 +361,15 @@
             cot_copy(d).start()
         up_push.start()
 
-    @pl.when(s >= LATE)
+    @pl.when(second)
+    def _():
+        pl.semaphore_signal(go, inc=1, device_id=(after, c), device_id_type=MESH)
+
+    @pl.when(first)
+    def _():
+        pl.semaphore_wait(go, 1)
+
+    @pl.when(late)
     def _():
         for d in far:
             x_copy(d).start()
@@ -445,7 +462,8 @@
             dma,
         ]
         + [dma((count,)) for _ in range(11)]
-        + [dma for _ in range(4)],
+        + [dma for _ in range(4)]
+        + [pltpu.SemaphoreType.REGULAR],
         compiler_params=pltpu.CompilerParams(
             collective_id=0, has_side_effects=True, vmem_limit_bytes=58 * 1024 * 1024
         ),

time: 229 us -> 179 us (0.78)
  Pallas kernels: 217 us -> 167 us
    pallas_call x1, Pallas kernels: 217 us -> 167 us  [per_device(): pl.pallas_call(kernel, out_shape=(jax.ShapeDtypeStruct((BLOCK, width), BF...]
where the time goes in v3:
time: 179 us
  Pallas kernels  167 us (93%)
  local copies, waits for them, and re-layouts  8.13 us (5%)
  other arithmetic  3.01 us (2%)
    pallas_call x1, Pallas kernels, per_device(): pl.pallas_call(kernel, out_shape=(jax.ShapeDtypeStruct((BLOCK, width), BF...  167 us
    unnamed x5, local copies, waits for them, and re-layouts  5.34 us

profile of v3, /device:TPU:0, one launch (start us, length us, event | category | flops | bytes accessed | tf_op | source)
XLA Modules:
  0.0 178.9 jit_solution(8338791098297905018)
XLA Ops:
  0.6 0.0 copy-start
  0.6 0.7 copy-done
  1.3 0.1 dynamic-slice_bitcast_fusion
  1.4 0.7 copy.16
  2.1 0.2 convert_reduce_fusion.1
  2.3 0.1 fusion.2
  2.4 0.1 select_reduce_fusion
  2.6 0.6 pad_add_fusion.order_ref
  3.2 0.1 add_compare_fusion
  3.3 0.6 add_convert_fusion.keep_ref
  3.9 0.7 copy.12.blocks_ref
  4.5 1.3 fusion.3
  5.8 0.7 broadcast_in_dim.24.gain_ref
  6.5 1.3 copy.13.col_ref
  7.9 167.1 %shard_map.86 = (bf16[128,1024]{1,0:T(8,128)(2,1)}, f32[256,1024]{1,0:T(8,128)}) custom-call(s32[16,3]{1,0:T(8,128)} %copy.12.blocks_ref, s32[2,16]{1,0:T(2,128)} %pad_add_fusion.order_ref, f32[2,16]{1,0:T(2,128)} %add_convert_fusion.keep_ref, bf16[128,1024]{1,0:T(8,128)(2,1)} %bitcast.36, f32[64,128]{1,0:T(8,128)} %broadcast_in_dim.24.gain_ref, ...), custom_call_target="tpu_custom_call" | custom-call | flops 5000000000 | bytes 20000000 | tf_op jit(solution)/shard_map/pallas_call | solution.py:418
  174.9 1.7 copy.19
  176.6 2.3 %copy.20 = f32[1,256,1024]{2,1,0:T(8,128)} copy(f32[1,256,1024]{2,1,0:T(8,128)} %bitcast.26) | data formatting | bytes 2097152
  (3 shorter events, 0.0 us)
Async XLA Ops:
  0.6 0.7 copy-start

commit v4 on v3

--- a/solution.py
+++ b/solution.py
@@ -15,18 +15,19 @@
 BF16 = jnp.bfloat16
 
 
-def segment_plan(third):
+def segment_plan(blocks):
+    third = blocks[:, 2]
     count = third.shape[0]
     ids = jnp.arange(count, dtype=jnp.int32)
     before = (third[None, :] < third[:, None]) | ((third[None, :] == third[:, None]) & (ids[None, :] < ids[:, None]))
     place = jnp.sum(before.astype(jnp.int32), axis=1)
     order = jnp.sum(jnp.where(place[None, :] == ids[:, None], ids[None, :], 0), axis=1)
     ordered = jnp.sum(jnp.where(place[None, :] == ids[:, None], third[None, :], 0), axis=1)
-    keep = (ordered == jnp.concatenate([ordered[:1] - 1, ordered[:-1]])).astype(F32)
+    keep = (ordered == jnp.concatenate([ordered[:1] - 1, ordered[:-1]])).astype(jnp.int32)
     upto = jnp.sum((third[None, :] <= ids[:, None]).astype(jnp.int32), axis=1)
-    has = jnp.any(third[None, :] == ids[:, None], axis=1).astype(F32)
+    has = jnp.any(third[None, :] == ids[:, None], axis=1).astype(jnp.int32)
     last = jnp.maximum(upto - 1, 0)
-    return jnp.stack([order, last]), jnp.stack([keep, has])
+    return jnp.concatenate([blocks.T, jnp.stack([order, last, keep, has])], axis=0)
 
 
 def dot(left, right):
@@ -42,10 +43,10 @@
 
 
 def kernel(
-    blocks_ref, order_ref, keep_ref, up_ref, gain_ref, row_ref, col_ref, x_ref, wi_ref, wo_ref,
+    plan_ref, up_ref, gain_ref, row_ref, x_ref, wi_ref, wo_ref,
     sg_ref, dw_ref,
     xv, xt, wi, wo_own, wo_next, psend, pin, xall, gate, query, key, value, keyt, valuet, weight, slope,
-    ahead, normed, fac, upbuf, sgsend, cotfirst, cotsend, cotin, gpa, gpb, gain_a, gain_b, gvt, gkt, segv, segk, acc,
+    ahead, normed, fac, col, upbuf, sgsend, cotfirst, cotsend, cotin, gpa, gpb, gain_a, gain_b, gvt, gkt, segv, segk, acc,
     xl, wil, wol, ps, pr, fs, cs, cr, as_, ar, bs, br, xs, xr, us, ur, ws, wr, go,
 ):
     count, _, width = xall.shape
@@ -165,6 +166,12 @@
             first_copy(d).start()
         cotin[c] = cotfirst[c]
         upbuf[...] = up_ref[...]
+
+    def spread(m, carry):
+        col[m] = jnp.broadcast_to(row_ref[m].astype(F32), (BLOCK, BLOCK)).T
+        return carry
+
+    lax.fori_loop(0, count, spread, 0)
 
     def x_copy(d):
         h = to(d)
@@ -207,20 +214,20 @@
 
     xall[c] = xv[...]
     scale = HD ** (-0.5)
-    gain = gain_ref[...]
+    gain = jnp.broadcast_to(gain_ref[c], (BLOCK, HD)).T
     apart = lax.broadcasted_iota(jnp.int32, (BLOCK, BLOCK), 0) - lax.broadcasted_iota(jnp.int32, (BLOCK, BLOCK), 1)
 
     def slots(n):
-        return [blocks_ref[n, t] for t in range(3)]
+        return [plan_ref[t, n] for t in range(3)]
 
     def attend(n, carry):
         listed = slots(n)
         at = [jnp.maximum(b, 0) for b in listed]
         scores = dot(jnp.concatenate([keyt[m] for m in at], axis=0), query[n]) * scale
-        rank = row_ref[n]
+        rank = row_ref[n].astype(F32)
         allowed = jnp.concatenate(
             [
-                (apart <= (n - b) * BLOCK) & (col_ref[m] == jnp.where(b >= 0, rank, -1.0))
+                (apart <= (n - b) * BLOCK) & (col[m] == jnp.where(b >= 0, rank, -1.0))
                 for b, m in zip(listed, at)
             ],
             axis=0,
@@ -263,7 +270,7 @@
         gvt[n] = ntdot(ga, weight[n])
         gkt[n] = ntdot(query[n], gs)
 
-    group = 4
+    group = 2
     for g in range(0, count, group):
         for d in near[g : g + group]:
             if d:
@@ -283,8 +290,8 @@
 
     def seg_step(i, carry):
         run_v, run_k = carry
-        n = order_ref[0, i]
-        keep = keep_ref[0, i]
+        n = plan_ref[3, i]
+        keep = plan_ref[5, i].astype(F32)
         run_v = run_v * keep + gvt[n, :, 2 * BLOCK :]
         run_k = run_k * keep + gkt[n, :, 2 * BLOCK :]
         segv[i] = run_v
@@ -297,8 +304,8 @@
     def finalise(d):
         m = source(d)
         later = lax.rem(m + 1, count)
-        last = order_ref[1, m]
-        has = keep_ref[1, m]
+        last = plan_ref[4, m]
+        has = plan_ref[6, m].astype(F32)
         gv = gvt[m, :, :BLOCK] + gvt[later, :, BLOCK : 2 * BLOCK] + segv[last] * has
         gk = gkt[m, :, :BLOCK] + gkt[later, :, BLOCK : 2 * BLOCK] + segk[last] * has
         gpb[m, :HD] = (gv * fac[m, 2]).astype(BF16)
@@ -334,7 +341,7 @@
         wo_push.wait_send()
     acc[...] = upbuf[...].astype(F32) + tdot(left, half_weights((0, 2), slice(None)))
 
-    @pl.when(jnp.logical_not(late))
+    @pl.when(s == 0)
     def _():
         weight_grad()
 
@@ -357,7 +364,7 @@
     @pl.when(s > 0)
     def _():
         set_cot(cotsend, dot(sgsend[...], wo_next[...]))
-        for d in far + [0]:
+        for d in near:
             cot_copy(d).start()
         up_push.start()
 
@@ -373,6 +380,9 @@
     def _():
         for d in far:
             x_copy(d).start()
+
+    @pl.when(s > 0)
+    def _():
         weight_grad()
 
     @pl.when(first)
@@ -395,14 +405,12 @@
 
 def per_device(key_blocks, ranker, section_inputs, output_grad, input_proj, output_proj, norm_gain):
     count = lax.axis_size("ctx")
-    c = lax.axis_index("ctx")
     x = section_inputs[0, 0]
     width = x.shape[1]
     blocks = key_blocks[0]
-    gain = lax.dynamic_slice_in_dim(norm_gain[0], c * HD, HD)
-    gain = jnp.broadcast_to(gain[:, None], (HD, BLOCK))
-    ranks = ranker[0].reshape(count, BLOCK).astype(F32)
-    order, keep = segment_plan(blocks[:, 2])
+    gain = norm_gain[0].reshape(count, 1, HD)
+    ranks = ranker[0].reshape(count, 1, BLOCK)
+    plan = segment_plan(blocks)
     vmem = pl.BlockSpec(memory_space=pltpu.VMEM)
     smem = pl.BlockSpec(memory_space=pltpu.SMEM)
     hbm = pl.BlockSpec(memory_space=pl.ANY)
@@ -421,7 +429,7 @@
             jax.ShapeDtypeStruct((BLOCK, width), BF16),
             jax.ShapeDtypeStruct((4 * HD, width), F32),
         ),
-        in_specs=[smem, smem, smem, vmem, vmem, vmem, vmem, hbm, hbm, hbm],
+        in_specs=[smem, vmem, vmem, vmem, hbm, hbm, hbm],
         out_specs=(vmem, vmem),
         scratch_shapes=[
             half(BLOCK, width),
@@ -443,6 +451,7 @@
             single(count, HD, BLOCK),
             single(count, HD, BLOCK),
             single(count, 4, HD, BLOCK),
+            single(count, BLOCK, BLOCK),
             half(BLOCK, width),
             half(BLOCK, width),
             half(count, HD, BLOCK),
@@ -469,7 +478,7 @@
         ),
         cost_estimate=pl.CostEstimate(flops=5 * 10**9, bytes_accessed=20 * 10**6, transcendentals=0),
     )(
-        blocks, order, keep, output_grad[0], gain, ranks[:, None, :], ranks[:, :, None],
+        plan, output_grad[0], gain, ranks,
         x, input_proj[0].reshape(count, 4, HD, width), output_proj[0],
     )
     return sg[None, None], dw[None]

time: 179 us -> 165 us (0.922)
  Pallas kernels: 167 us -> 155 us
    pallas_call x1, Pallas kernels: 167 us -> 155 us  [per_device(): pl.pallas_call(kernel, out_shape=(jax.ShapeDtypeStruct((BLOCK, width), BF...]
    unnamed x5 -> x4, local copies, waits for them, and re-layouts: 5.34 us -> 5.17 us
where the time goes in v4:
time: 165 us; the launch traced here: 164 us
  Pallas kernels  155 us (94%)
  local copies, waits for them, and re-layouts  6.46 us (4%)
  other arithmetic  1.89 us (1%)
    pallas_call x1, Pallas kernels, per_device(): pl.pallas_call(kernel, out_shape=(jax.ShapeDtypeStruct((BLOCK, width), BF...  155 us
    unnamed x4, local copies, waits for them, and re-layouts  5.17 us

profile of v4, /device:TPU:0, one launch (start us, length us, event | category | flops | bytes accessed | tf_op | source)
XLA Modules:
  0.0 164.5 jit_solution(5348308862485442658)
XLA Ops:
  0.6 0.7 copy.12
  1.3 0.2 convert_reduce_fusion.1
  1.5 0.1 fusion.2
  1.6 0.1 select_reduce_fusion
  1.8 0.1 compare_convert_fusion
  1.9 0.6 concatenate.20.plan_ref
  2.5 0.5 broadcast.33
  3.1 1.3 reduce.3
  4.4 0.7 reshape_squeeze.9.gain_ref
  5.1 155.4 %shard_map.86 = (bf16[128,1024]{1,0:T(8,128)(2,1)}, f32[256,1024]{1,0:T(8,128)}) custom-call(s32[7,16]{1,0:T(8,128)} %concatenate.20.plan_ref, bf16[128,1024]{1,0:T(8,128)(2,1)} %bitcast.34, f32[16,1,64]{2,1,0:T(1,128)} %reshape_squeeze.9.gain_ref, s32[16,1,128]{2,1,0:T(1,128)} %bitcast.36, bf16[128,1024]{1,0:T(8,128)(2,1)} %bitcast.35, ...), custom_call_target="tpu_custom_call" | custom-call | flops 5000000000 | bytes 20000000 | tf_op jit(solution)/shard_map/pallas_call | solution.py:426
  160.5 1.7 %copy.15 = bf16[1,1,128,1024]{3,2,1,0:T(8,128)(2,1)} copy(bf16[1,1,128,1024]{3,2,1,0:T(8,128)(2,1)} %bitcast.27) | data formatting | bytes 524288
  162.2 2.3 %copy.16 = f32[1,256,1024]{2,1,0:T(8,128)} copy(f32[1,256,1024]{2,1,0:T(8,128)} %bitcast.26) | data formatting | bytes 2097152
  (4 shorter events, 0.0 us)

commit v5 on v4

--- a/solution.py
+++ b/solution.py
@@ -46,8 +46,8 @@
     plan_ref, up_ref, gain_ref, row_ref, x_ref, wi_ref, wo_ref,
     sg_ref, dw_ref,
     xv, xt, wi, wo_own, wo_next, psend, pin, xall, gate, query, key, value, keyt, valuet, weight, slope,
-    ahead, normed, fac, col, upbuf, sgsend, cotfirst, cotsend, cotin, gpa, gpb, gain_a, gain_b, gvt, gkt, segv, segk, acc,
-    xl, wil, wol, ps, pr, fs, cs, cr, as_, ar, bs, br, xs, xr, us, ur, ws, wr, go,
+    ahead, normed, fac, col, upbuf, sgsend, cotfirst, cotsend, cotin, cotown, open_send, open_all, gpa, gpb, gain_a, gain_b, gvt, gkt, segv, segk, acc,
+    xl, wil, wol, ps, pr, fs, cs, cr, as_, ar, bs, br, xs, xr, us, ur, ws, wr, os_, or_, gs_, gr, go,
 ):
     count, _, width = xall.shape
     side = math.isqrt(count)
@@ -104,6 +104,23 @@
         pl.semaphore_signal(barrier, inc=1, device_id=(s, to(d)), device_id_type=MESH)
     for h in range(count):
         pl.semaphore_signal(barrier, inc=1, device_id=(after, h), device_id_type=MESH)
+    def set_cot(held, cot):
+        held[...] = cot.T.astype(BF16).reshape(count, HD, BLOCK)
+
+    def spread(m, carry):
+        col[m] = jnp.broadcast_to(row_ref[m].astype(F32), (BLOCK, BLOCK)).T
+        return carry
+
+    lax.fori_loop(0, count, spread, 0)
+
+    x_load.wait()
+    xt[...] = xv[...].T
+
+    @pl.when(first)
+    def _():
+        wo_load.wait()
+        set_cot(cotfirst, dot(up_ref[...], wo_own[...]))
+
     pl.semaphore_wait(barrier, 2 * count)
 
     wo_push = remote(wo_ref, wo_next, ws, wr, (after, c))
@@ -124,17 +141,12 @@
         n = source(d)
         return remote(cotsend.at[n], cotin.at[n], cs.at[d], cr.at[d], (s, n))
 
-    def set_cot(held, cot):
-        held[...] = cot.T.astype(BF16).reshape(count, HD, BLOCK)
-
     def p_copy(h):
         return remote(psend.at[h], pin.at[c], ps.at[h], pr.at[c], (s, h))
 
     def p_arrival(h):
         return remote(psend.at[h], pin.at[h], ps.at[h], pr.at[h], (s, h))
 
-    x_load.wait()
-    xt[...] = xv[...].T
 
     def project(i, carry):
         k = chunk_at(i)
@@ -160,18 +172,10 @@
 
     @pl.when(first)
     def _():
-        wo_load.wait()
-        set_cot(cotfirst, dot(up_ref[...], wo_own[...]))
         for d in far:
             first_copy(d).start()
         cotin[c] = cotfirst[c]
         upbuf[...] = up_ref[...]
-
-    def spread(m, carry):
-        col[m] = jnp.broadcast_to(row_ref[m].astype(F32), (BLOCK, BLOCK)).T
-        return carry
-
-    lax.fori_loop(0, count, spread, 0)
 
     def x_copy(d):
         h = to(d)
@@ -241,7 +245,9 @@
         norm = attended * inv_rms
         normed[n] = norm
         ahead[n] = inv_rms * gain * gate[n].astype(F32)
-        fac[n, 0] = gain * norm * fac[n, 0]
+        opening = gain * norm * fac[n, 0]
+        fac[n, 0] = opening
+        open_send[n] = opening.astype(BF16)
         return carry
 
     lax.fori_loop(0, count, attend, 0, unroll=2)
@@ -250,9 +256,21 @@
         n = source(d)
         return remote(src.at[n], landing.at[c], send.at[d], recv.at[d], (s, n))
 
+    def query_copy(d):
+        n = source(d)
+        return remote(gpa.at[n, pl.ds(HD, HD)], gain_a.at[c], as_.at[d], ar.at[d], (s, n))
+
+    def query_arrival(d):
+        h = to(d)
+        return remote(gpa.at[h, pl.ds(HD, HD)], gain_a.at[h], as_.at[d], ar.at[d], (s, h))
+
     def back_arrival(src, landing, send, recv, d):
         h = to(d)
         return remote(src.at[h], landing.at[h], send.at[d], recv.at[d], (s, h))
+
+    for d in far:
+        back_copy(open_send, open_all, gs_, gr, d).start()
+    open_all[c] = open_send[c]
 
     def head(d):
         n = source(d)
@@ -285,8 +303,8 @@
             head(d)
         for d in near[g : g + group]:
             if d:
-                back_copy(gpa, gain_a, as_, ar, d).start()
-    gain_a[c] = gpa[c]
+                query_copy(d).start()
+    gain_a[c] = gpa[c, HD:]
 
     def seg_step(i, carry):
         run_v, run_k = carry
@@ -331,15 +349,26 @@
     def half_weights(parts, span):
         return jnp.concatenate([wi[h, p, :, span] for h in range(count) for p in parts], axis=0)
 
+    own_push = remote(cotsend, cotown, os_, or_, (before, c))
+
     for d in near[1:]:
-        back_arrival(gpa, gain_a, as_, ar, d).wait_recv()
-    left = gain_a[...].reshape(count * BLOCK, BLOCK)
+        back_arrival(open_send, open_all, gs_, gr, d).wait_recv()
 
     @pl.when(jnp.logical_not(first))
     def _():
         remote(sgsend, upbuf, us, ur, (s, c)).wait_recv()
+        remote(cotsend, cotown, os_, or_, (s, c)).wait_recv()
         wo_push.wait_send()
-    acc[...] = upbuf[...].astype(F32) + tdot(left, half_weights((0, 2), slice(None)))
+
+    @pl.when(first)
+    def _():
+        cotown[...] = cotfirst[...]
+
+    opened = (cotown[...].astype(F32) * open_all[...].astype(F32)).astype(BF16).reshape(count * HD, BLOCK)
+    acc[...] = upbuf[...].astype(F32) + tdot(opened, half_weights((0,), slice(None)))
+    for d in near[1:]:
+        query_arrival(d).wait_recv()
+    acc[...] += tdot(gain_a[...].reshape(count * HD, BLOCK), half_weights((2,), slice(None)))
 
     @pl.when(s == 0)
     def _():
@@ -367,6 +396,7 @@
         for d in near:
             cot_copy(d).start()
         up_push.start()
+        own_push.start()
 
     @pl.when(second)
     def _():
@@ -392,7 +422,8 @@
 
     for d in far:
         p_copy(to(d)).wait_send()
-        back_copy(gpa, gain_a, as_, ar, d).wait_send()
+        query_copy(d).wait_send()
+        back_copy(open_send, open_all, gs_, gr, d).wait_send()
         back_copy(gpb, gain_b, bs, br, d).wait_send()
         x_copy(d).wait_send()
 
@@ -401,6 +432,7 @@
         for d in far + [0]:
             cot_copy(d).wait_send()
         up_push.wait_send()
+        own_push.wait_send()
 
 
 def per_device(key_blocks, ranker, section_inputs, output_grad, input_proj, output_proj, norm_gain):
@@ -457,9 +489,12 @@
             half(count, HD, BLOCK),
             half(count, HD, BLOCK),
             half(count, HD, BLOCK),
+            half(count, HD, BLOCK),
+            half(count, HD, BLOCK),
+            half(count, HD, BLOCK),
             half(count, 2 * HD, BLOCK),
             half(count, 2 * HD, BLOCK),
-            half(count, 2 * HD, BLOCK),
+            half(count, HD, BLOCK),
             half(count, 2 * HD, BLOCK),
             single(count, HD, full),
             single(count, HD, full),
@@ -471,7 +506,8 @@
             dma,
         ]
         + [dma((count,)) for _ in range(11)]
-        + [dma for _ in range(4)]
+        + [dma for _ in range(6)]
+        + [dma((count,)) for _ in range(2)]
         + [pltpu.SemaphoreType.REGULAR],
         compiler_params=pltpu.CompilerParams(
             collective_id=0, has_side_effects=True, vmem_limit_bytes=58 * 1024 * 1024

time: 165 us -> 162 us (0.982)
  Pallas kernels: 155 us -> 153 us
    pallas_call x1, Pallas kernels: 155 us -> 153 us  [per_device(): pl.pallas_call(kernel, out_shape=(jax.ShapeDtypeStruct((BLOCK, width), BF...]
where the time goes in v5:
time: 162 us
  Pallas kernels  153 us (94%)
  local copies, waits for them, and re-layouts  6.46 us (4%)
  other arithmetic  1.89 us (1%)
    pallas_call x1, Pallas kernels, per_device(): pl.pallas_call(kernel, out_shape=(jax.ShapeDtypeStruct((BLOCK, width), BF...  153 us
    unnamed x4, local copies, waits for them, and re-layouts  5.17 us

profile of v5, /device:TPU:0, one launch (start us, length us, event | category | flops | bytes accessed | tf_op | source)
XLA Modules:
  0.0 162.2 jit_solution(6697121258236680168)
XLA Ops:
  0.6 0.7 copy.12
  1.3 0.2 convert_reduce_fusion.1
  1.5 0.1 fusion.2
  1.6 0.1 select_reduce_fusion
  1.8 0.1 compare_convert_fusion
  1.9 0.6 concatenate.20.plan_ref
  2.5 0.5 broadcast.33
  3.1 1.3 reduce.3
  4.4 0.7 reshape_squeeze.9.gain_ref
  5.1 153.1 %shard_map.86 = (bf16[128,1024]{1,0:T(8,128)(2,1)}, f32[256,1024]{1,0:T(8,128)}) custom-call(s32[7,16]{1,0:T(8,128)} %concatenate.20.plan_ref, bf16[128,1024]{1,0:T(8,128)(2,1)} %bitcast.34, f32[16,1,64]{2,1,0:T(1,128)} %reshape_squeeze.9.gain_ref, s32[16,1,128]{2,1,0:T(1,128)} %bitcast.36, bf16[128,1024]{1,0:T(8,128)(2,1)} %bitcast.35, ...), custom_call_target="tpu_custom_call" | custom-call | flops 5000000000 | bytes 20000000 | tf_op jit(solution)/shard_map/pallas_call | solution.py:458
  158.2 1.7 %copy.15 = bf16[1,1,128,1024]{3,2,1,0:T(8,128)(2,1)} copy(bf16[1,1,128,1024]{3,2,1,0:T(8,128)(2,1)} %bitcast.27) | data formatting | bytes 524288
  159.9 2.3 %copy.16 = f32[1,256,1024]{2,1,0:T(8,128)} copy(f32[1,256,1024]{2,1,0:T(8,128)} %bitcast.26) | data formatting | bytes 2097152
  (4 shorter events, 0.0 us)

commit v6 on v5

--- a/solution.py
+++ b/solution.py
@@ -15,21 +15,6 @@
 BF16 = jnp.bfloat16
 
 
-def segment_plan(blocks):
-    third = blocks[:, 2]
-    count = third.shape[0]
-    ids = jnp.arange(count, dtype=jnp.int32)
-    before = (third[None, :] < third[:, None]) | ((third[None, :] == third[:, None]) & (ids[None, :] < ids[:, None]))
-    place = jnp.sum(before.astype(jnp.int32), axis=1)
-    order = jnp.sum(jnp.where(place[None, :] == ids[:, None], ids[None, :], 0), axis=1)
-    ordered = jnp.sum(jnp.where(place[None, :] == ids[:, None], third[None, :], 0), axis=1)
-    keep = (ordered == jnp.concatenate([ordered[:1] - 1, ordered[:-1]])).astype(jnp.int32)
-    upto = jnp.sum((third[None, :] <= ids[:, None]).astype(jnp.int32), axis=1)
-    has = jnp.any(third[None, :] == ids[:, None], axis=1).astype(jnp.int32)
-    last = jnp.maximum(upto - 1, 0)
-    return jnp.concatenate([blocks.T, jnp.stack([order, last, keep, has])], axis=0)
-
-
 def dot(left, right):
     return jnp.dot(left, right, preferred_element_type=F32)
 
@@ -43,11 +28,11 @@
 
 
 def kernel(
-    plan_ref, up_ref, gain_ref, row_ref, x_ref, wi_ref, wo_ref,
+    blocks_ref, up_ref, gain_ref, row_ref, x_ref, wi_ref, wo_ref,
     sg_ref, dw_ref,
     xv, xt, wi, wo_own, wo_next, psend, pin, xall, gate, query, key, value, keyt, valuet, weight, slope,
     ahead, normed, fac, col, upbuf, sgsend, cotfirst, cotsend, cotin, cotown, open_send, open_all, gpa, gpb, gain_a, gain_b, gvt, gkt, segv, segk, acc,
-    xl, wil, wol, ps, pr, fs, cs, cr, as_, ar, bs, br, xs, xr, us, ur, ws, wr, os_, or_, gs_, gr, go,
+    xl, wil, wol, ps, pr, fs, cs, cr, as_, ar, bs, br, xs, xr, us, ur, ws, wr, os_, or_, gs_, gr, go, chain,
 ):
     count, _, width = xall.shape
     side = math.isqrt(count)
@@ -71,6 +56,7 @@
         return min(y, side - y) + min(z, side - z)
 
     near = sorted(range(count), key=distance)
+    spiral = sorted(range(side), key=lambda v: min(v, side - v))
     far = [d for d in near[::-1] if d]
 
     def remote(src, dst, send, recv, where):
@@ -112,6 +98,19 @@
         return carry
 
     lax.fori_loop(0, count, spread, 0)
+
+    newest = [jnp.int32(-1)] * count
+    for n in range(count):
+        read = blocks_ref[n, 2]
+        prior = jnp.int32(-1)
+        for m in range(n):
+            prior = jnp.where(read == m, newest[m], prior)
+            newest[m] = jnp.where(read == m, n, newest[m])
+        chain[0, n] = prior
+    for m in range(count):
+        chain[1, m] = newest[m]
+    segv[...] = jnp.zeros_like(segv)
+    segk[...] = jnp.zeros_like(segk)
 
     x_load.wait()
     xt[...] = xv[...].T
@@ -222,7 +221,7 @@
     apart = lax.broadcasted_iota(jnp.int32, (BLOCK, BLOCK), 0) - lax.broadcasted_iota(jnp.int32, (BLOCK, BLOCK), 1)
 
     def slots(n):
-        return [plan_ref[t, n] for t in range(3)]
+        return [blocks_ref[n, t] for t in range(3)]
 
     def attend(n, carry):
         listed = slots(n)
@@ -306,24 +305,22 @@
                 query_copy(d).start()
     gain_a[c] = gpa[c, HD:]
 
-    def seg_step(i, carry):
-        run_v, run_k = carry
-        n = plan_ref[3, i]
-        keep = plan_ref[5, i].astype(F32)
-        run_v = run_v * keep + gvt[n, :, 2 * BLOCK :]
-        run_k = run_k * keep + gkt[n, :, 2 * BLOCK :]
-        segv[i] = run_v
-        segk[i] = run_k
-        return run_v, run_k
-
-    zero = jnp.zeros((HD, BLOCK), F32)
-    lax.fori_loop(0, count, seg_step, (zero, zero), unroll=2)
+    def seg_step(n, carry):
+        prior = chain[0, n]
+        back = jnp.maximum(prior, 0)
+        keep = (prior >= 0).astype(F32)
+        segv[n] = segv[back] * keep + gvt[n, :, 2 * BLOCK :]
+        segk[n] = segk[back] * keep + gkt[n, :, 2 * BLOCK :]
+        return carry
+
+    lax.fori_loop(0, count, seg_step, 0, unroll=2)
 
     def finalise(d):
         m = source(d)
         later = lax.rem(m + 1, count)
-        last = plan_ref[4, m]
-        has = plan_ref[6, m].astype(F32)
+        newest = chain[1, m]
+        last = jnp.maximum(newest, 0)
+        has = (newest >= 0).astype(F32)
         gv = gvt[m, :, :BLOCK] + gvt[later, :, BLOCK : 2 * BLOCK] + segv[last] * has
         gk = gkt[m, :, :BLOCK] + gkt[later, :, BLOCK : 2 * BLOCK] + segk[last] * has
         gpb[m, :HD] = (gv * fac[m, 2]).astype(BF16)
@@ -392,9 +389,13 @@
 
     @pl.when(s > 0)
     def _():
-        set_cot(cotsend, dot(sgsend[...], wo_next[...]))
-        for d in near:
-            cot_copy(d).start()
+        for dy in spiral:
+            k = lax.rem(cy + dy, side)
+            cols = pl.ds(pl.multiple_of(k * side * HD, side * HD), side * HD)
+            part = dot(sgsend[...], wo_next[:, cols])
+            cotsend[pl.ds(k * side, side)] = part.T.astype(BF16).reshape(side, HD, BLOCK)
+            for dz in spiral:
+                cot_copy(dy * side + dz).start()
         up_push.start()
         own_push.start()
 
@@ -442,7 +443,6 @@
     blocks = key_blocks[0]
     gain = norm_gain[0].reshape(count, 1, HD)
     ranks = ranker[0].reshape(count, 1, BLOCK)
-    plan = segment_plan(blocks)
     vmem = pl.BlockSpec(memory_space=pltpu.VMEM)
     smem = pl.BlockSpec(memory_space=pltpu.SMEM)
     hbm = pl.BlockSpec(memory_space=pl.ANY)
@@ -508,13 +508,13 @@
         + [dma((count,)) for _ in range(11)]
         + [dma for _ in range(6)]
         + [dma((count,)) for _ in range(2)]
-        + [pltpu.SemaphoreType.REGULAR],
+        + [pltpu.SemaphoreType.REGULAR, pltpu.SMEM((2, count), jnp.int32)],
         compiler_params=pltpu.CompilerParams(
             collective_id=0, has_side_effects=True, vmem_limit_bytes=58 * 1024 * 1024
         ),
         cost_estimate=pl.CostEstimate(flops=5 * 10**9, bytes_accessed=20 * 10**6, transcendentals=0),
     )(
-        plan, output_grad[0], gain, ranks,
+        blocks, output_grad[0], gain, ranks,
         x, input_proj[0].reshape(count, 4, HD, width), output_proj[0],
     )
     return sg[None, None], dw[None]

time: 162 us -> 161 us (level)
    unnamed x4 -> x3, local copies, waits for them, and re-layouts: 5.17 us -> 4.49 us
where the time goes in v6:
time: 161 us
  Pallas kernels  153 us (95%)
  local copies, waits for them, and re-layouts  6.52 us (4%)
    pallas_call x1, Pallas kernels, per_device(): pl.pallas_call(kernel, out_shape=(jax.ShapeDtypeStruct((BLOCK, width), BF...  153 us
    unnamed x3, local copies, waits for them, and re-layouts  4.49 us

profile of v6, /device:TPU:0, one launch (start us, length us, event | category | flops | bytes accessed | tf_op | source)
XLA Modules:
  0.0 161.2 jit_solution(15148246818545174961)
XLA Ops:
  0.6 0.5 broadcast.3
  1.1 1.3 reduce.3
  2.5 0.7 reshape_squeeze.9.gain_ref
  3.2 1.4 copy.10
  4.5 152.7 %shard_map.86 = (bf16[128,1024]{1,0:T(8,128)(2,1)}, f32[256,1024]{1,0:T(8,128)}) custom-call(s32[16,3]{1,0:T(8,128)} %bitcast.10, bf16[128,1024]{1,0:T(8,128)(2,1)} %bitcast.13, f32[16,1,64]{2,1,0:T(1,128)} %reshape_squeeze.9.gain_ref, s32[16,1,128]{2,1,0:T(1,128)} %bitcast.15, bf16[128,1024]{1,0:T(8,128)(2,1)} %bitcast.14, ...), custom_call_target="tpu_custom_call" | custom-call | flops 5000000000 | bytes 20000000 | tf_op jit(solution)/shard_map/pallas_call | solution.py:458
  157.2 1.7 %copy.13 = bf16[1,1,128,1024]{3,2,1,0:T(8,128)(2,1)} copy(bf16[1,1,128,1024]{3,2,1,0:T(8,128)(2,1)} %bitcast.9) | data formatting | bytes 524288
  158.9 2.3 %copy.14 = f32[1,256,1024]{2,1,0:T(8,128)} copy(f32[1,256,1024]{2,1,0:T(8,128)} %bitcast.8) | data formatting | bytes 2097152

commit v7 on v6

--- a/solution.py
+++ b/solution.py
@@ -237,7 +237,7 @@
         )
         sigma = jax.nn.sigmoid(scores)
         now = jnp.where(allowed, scores * sigma, 0.0).astype(BF16)
-        weight[n] = now
+        weight[n] = now.astype(F32).T.astype(BF16)
         slope[n] = (jnp.where(allowed, sigma * (1.0 + scores * (1.0 - sigma)), 0.0) * scale).astype(BF16)
         attended = dot(jnp.concatenate([value[m] for m in at], axis=1), now)
         inv_rms = lax.rsqrt(jnp.sum(attended * attended, axis=0, keepdims=True) * (1.0 / HD) + 1.0)
@@ -284,7 +284,7 @@
         gq = dot(jnp.concatenate([key[m] for m in at], axis=1), gs)
         gpa[n, :HD] = (cot_n * fac[n, 0]).astype(BF16)
         gpa[n, HD:] = (gq * fac[n, 1]).astype(BF16)
-        gvt[n] = ntdot(ga, weight[n])
+        gvt[n] = dot(ga, weight[n])
         gkt[n] = ntdot(query[n], gs)
 
     group = 2
@@ -478,7 +478,7 @@
             half(count, HD, BLOCK),
             half(count, BLOCK, HD),
             half(count, BLOCK, HD),
-            half(count, full, BLOCK),
+            half(count, BLOCK, full),
             half(count, full, BLOCK),
             single(count, HD, BLOCK),
             single(count, HD, BLOCK),

time: 161 us -> 161 us (level)
  no operation moved by 1% of the time
where the time goes in v7:
time: 161 us
  Pallas kernels  152 us (94%)
  local copies, waits for them, and re-layouts  6.52 us (4%)
    pallas_call x1, Pallas kernels, per_device(): pl.pallas_call(kernel, out_shape=(jax.ShapeDtypeStruct((BLOCK, width), BF...  152 us
    unnamed x3, local copies, waits for them, and re-layouts  4.49 us

profile of v7, /device:TPU:0, one launch (start us, length us, event | category | flops | bytes accessed | tf_op | source)
XLA Modules:
  0.0 160.8 jit_solution(15525714790884562244)
XLA Ops:
  0.6 0.5 broadcast.3
  1.1 1.3 reduce.3
  2.5 0.7 reshape_squeeze.9.gain_ref
  3.2 1.4 copy.10
  4.5 152.3 %shard_map.86 = (bf16[128,1024]{1,0:T(8,128)(2,1)}, f32[256,1024]{1,0:T(8,128)}) custom-call(s32[16,3]{1,0:T(8,128)} %bitcast.10, bf16[128,1024]{1,0:T(8,128)(2,1)} %bitcast.13, f32[16,1,64]{2,1,0:T(1,128)} %reshape_squeeze.9.gain_ref, s32[16,1,128]{2,1,0:T(1,128)} %bitcast.15, bf16[128,1024]{1,0:T(8,128)(2,1)} %bitcast.14, ...), custom_call_target="tpu_custom_call" | custom-call | flops 5000000000 | bytes 20000000 | tf_op jit(solution)/shard_map/pallas_call | solution.py:458
  156.8 1.7 %copy.13 = bf16[1,1,128,1024]{3,2,1,0:T(8,128)(2,1)} copy(bf16[1,1,128,1024]{3,2,1,0:T(8,128)(2,1)} %bitcast.9) | data formatting | bytes 524288
  158.5 2.3 %copy.14 = f32[1,256,1024]{2,1,0:T(8,128)} copy(f32[1,256,1024]{2,1,0:T(8,128)} %bitcast.8) | data formatting | bytes 2097152

commit v8 on v6

--- a/solution.py
+++ b/solution.py
@@ -249,7 +249,7 @@
         open_send[n] = opening.astype(BF16)
         return carry
 
-    lax.fori_loop(0, count, attend, 0, unroll=2)
+    lax.fori_loop(0, count, attend, 0, unroll=4)
 
     def back_copy(src, landing, send, recv, d):
         n = source(d)

time: 161 us -> 162 us (level)
  no operation moved by 1% of the time
where the time goes in v8:
time: 162 us
  Pallas kernels  153 us (94%)
  local copies, waits for them, and re-layouts  6.52 us (4%)
    pallas_call x1, Pallas kernels, per_device(): pl.pallas_call(kernel, out_shape=(jax.ShapeDtypeStruct((BLOCK, width), BF...  153 us
    unnamed x3, local copies, waits for them, and re-layouts  4.49 us

profile of v8, /device:TPU:0, one launch (start us, length us, event | category | flops | bytes accessed | tf_op | source)
XLA Modules:
  0.0 161.8 jit_solution(13754587025133042575)
XLA Ops:
  0.6 0.5 broadcast.3
  1.1 1.3 reduce.3
  2.5 0.7 reshape_squeeze.9.gain_ref
  3.2 1.4 copy.10
  4.5 153.3 %shard_map.86 = (bf16[128,1024]{1,0:T(8,128)(2,1)}, f32[256,1024]{1,0:T(8,128)}) custom-call(s32[16,3]{1,0:T(8,128)} %bitcast.10, bf16[128,1024]{1,0:T(8,128)(2,1)} %bitcast.13, f32[16,1,64]{2,1,0:T(1,128)} %reshape_squeeze.9.gain_ref, s32[16,1,128]{2,1,0:T(1,128)} %bitcast.15, bf16[128,1024]{1,0:T(8,128)(2,1)} %bitcast.14, ...), custom_call_target="tpu_custom_call" | custom-call | flops 5000000000 | bytes 20000000 | tf_op jit(solution)/shard_map/pallas_call | solution.py:458
  157.8 1.7 %copy.13 = bf16[1,1,128,1024]{3,2,1,0:T(8,128)(2,1)} copy(bf16[1,1,128,1024]{3,2,1,0:T(8,128)(2,1)} %bitcast.9) | data formatting | bytes 524288
  159.5 2.3 %copy.14 = f32[1,256,1024]{2,1,0:T(8,128)} copy(f32[1,256,1024]{2,1,0:T(8,128)} %bitcast.8) | data formatting | bytes 2097152
